TPU v7x, 512 devices: a whole 4x4x16 slice. The times are simulated.
512 devices in a mesh: cls: 64 (over x, z), ptl: 8 (over y, core).
Axes of the slice: x: 4, y: 4, z: 16, core: 2. Of those that a mesh axis runs over, the one named last changes fastest.
Arguments:
- images: float32 [128, 9216], P('ptl', 'cls'), may hold values from -13 to 13
- references: bfloat16 [256, 9216], P('cls'), may hold values from -6 to 6
- ctf_table: float32 [32, 32], replicated, may hold values from -1 to 1
- noise_inv: float32 [32, 32], replicated, may hold values from 0.003 to 0.30381945
- defocus_group: int32 [128], P('ptl'), may hold values from 0 to 31
- micrograph: int32 [128], P('ptl'), may hold values from 0 to 31, as said below
- batch_size: int32 [128], P('ptl'), may hold values from 0 to 16, as said below
Outputs:
- class_post: float32 [128, 256], P('ptl', 'cls')
- rot_post: float32 [128, 36], P('ptl')
Inputs may be any that keep to these rules, and one draw needn't show every extreme that they name: The slots of index i of ptl name micrographs i * 4 to (i + 1) * 4 - 1, and the micrograph number never decreases from one slot to the next; live slots of one micrograph are consecutive. On each index of ptl the live slots (batch_size > 0) come first; a live slot holds the number of live slots of its micrograph. Some index of ptl has all 16 slots live; every index has at least one.
All inputs are finite; a program needn't handle non-finite values.
Results may differ from a plain program's by a relative error of at most 0.0003.
Values sent between devices are 32-bit elements; how exact they have to be, the bound alone decides.
A program may use at most 128 MiB of HBM per device.

v0:
```python
import math

import jax
import jax.numpy as jnp
from jax import lax
from jax.sharding import PartitionSpec as P

CYCLES = 32
ANG = 144
ROT = 36
SHIFTS = 128
BOX = 128
PBLOCK = 4


def phase_table(cycles, angles, shifts, box):
    radius = (jnp.arange(cycles, dtype=jnp.float32) + 1.0) / box
    theta = jnp.arange(angles, dtype=jnp.float32) * (2.0 * math.pi / angles)
    index = jnp.arange(shifts, dtype=jnp.int32)
    shift_x = (index % 16 - 8).astype(jnp.float32)
    shift_y = (index // 16 - shifts // 32).astype(jnp.float32)
    along = jnp.cos(theta)[:, None] * shift_x[None, :] + jnp.sin(theta)[:, None] * shift_y[None, :]
    phase = 2.0 * math.pi * radius[:, None, None] * along[None, :, :]
    table = jnp.concatenate([jnp.cos(phase), jnp.sin(phase)], axis=0)
    return table.reshape(2 * cycles * angles, shifts).astype(jnp.bfloat16)


def rotate_all(refs, turns, stride):
    return jnp.stack([jnp.roll(refs, stride * turn, axis=-1) for turn in range(turns)], axis=1)


def body(images, references, ctf_table, noise_inv, defocus_group, micrograph, batch_size):
    labels = jnp.stack([defocus_group, micrograph, batch_size], axis=1)
    slots = images.shape[0]
    gathered = lax.all_gather(images, "cls", axis=1, tiled=True)
    groups = ctf_table.shape[0]
    mics = noise_inv.shape[0]
    pick_group = (labels[:, 0:1] == jnp.arange(groups, dtype=jnp.int32)[None, :]).astype(
        jnp.float32
    )
    pick_mic = (labels[:, 1:2] == jnp.arange(mics, dtype=jnp.int32)[None, :]).astype(jnp.float32)
    ctf_rows = jnp.dot(pick_group, ctf_table, precision=lax.Precision.HIGHEST)
    noise_rows = jnp.dot(pick_mic, noise_inv, precision=lax.Precision.HIGHEST)
    counted = labels[:, 2].astype(jnp.float32)
    shrink = counted / (counted + 1.0)
    weight = ctf_rows * noise_rows * shrink[:, None]
    local = references.shape[0]
    refs = references.astype(jnp.float32).reshape(local, 2, CYCLES, ANG)
    power = jnp.sum(refs * refs, axis=(1, 3))
    quad = 0.5 * jnp.dot(ctf_rows * weight, power.T, precision=lax.Precision.HIGHEST)
    rotated = rotate_all(refs, ROT, ANG // ROT)
    table = phase_table(CYCLES, ANG, SHIFTS, BOX)
    parts = gathered.reshape(slots, 2, CYCLES, ANG)
    real_z = parts[:, 0] * weight[:, :, None]
    imag_z = -parts[:, 1] * weight[:, :, None]
    blocks = slots // PBLOCK

    def score_block(item):
        zre, zim, offset, sizes = item

        def compute(unused):
            real_y = (
                zre[:, None, None] * rotated[None, :, :, 0]
                - zim[:, None, None] * rotated[None, :, :, 1]
            )
            imag_y = (
                zre[:, None, None] * rotated[None, :, :, 1]
                + zim[:, None, None] * rotated[None, :, :, 0]
            )
            product = (
                jnp.stack([real_y, imag_y], axis=3)
                .reshape(PBLOCK * local * ROT, 2 * CYCLES * ANG)
                .astype(jnp.bfloat16)
            )
            corr = jnp.dot(product, table, preferred_element_type=jnp.float32)
            logits = corr.reshape(PBLOCK, local, ROT, SHIFTS) - offset[:, :, None, None]
            return jax.nn.logsumexp(logits, axis=3)

        def skipped(unused):
            return jnp.zeros((PBLOCK, local, ROT), jnp.float32)

        return lax.cond(jnp.any(sizes > 0), compute, skipped, 0)

    scores = lax.map(
        score_block,
        (
            real_z.reshape(blocks, PBLOCK, CYCLES, ANG),
            imag_z.reshape(blocks, PBLOCK, CYCLES, ANG),
            quad.reshape(blocks, PBLOCK, local),
            labels[:, 2].reshape(blocks, PBLOCK),
        ),
    )
    scores = scores.reshape(slots, local, ROT)
    class_lse = jax.nn.logsumexp(scores, axis=2)
    peak = lax.pmax(jnp.max(scores, axis=1), "cls")
    total = lax.psum(jnp.sum(jnp.exp(scores - peak[:, None, :]), axis=1), "cls")
    rot_lse = peak + jnp.log(total)
    norm = jax.nn.logsumexp(rot_lse, axis=1)
    live = (labels[:, 2] > 0)[:, None]
    class_post = jnp.where(live, class_lse - norm[:, None], 0.0)
    rot_post = jnp.where(live, rot_lse - norm[:, None], 0.0)
    return (class_post, rot_post)


def solution(mesh):
    in_specs = (P("ptl", "cls"), P("cls", None), P(), P(), P("ptl"), P("ptl"), P("ptl"))
    out_specs = (P("ptl", "cls"), P("ptl", None))
    return jax.shard_map(body, mesh=mesh, in_specs=in_specs, out_specs=out_specs, check_vma=False)
```

profile of v0, /device:TPU:32, one launch (start us, length us, event | category | flops | bytes accessed | tf_op | source)
XLA Modules:
  0.0 687.2 jit_solution(3444561856658375457)
XLA Ops:
  17.0 9.0 %fusion.9 = (bf16[32,144,128]{2,1,0:T(8,128)(2,1)S(1)}, bf16[32,144,128]{2,1,0:T(8,128)(2,1)S(1)}) fusion(f32[144,128]{1,0:T(8,128)S(1)} %multiply_add_fusion, f32[32]{0:T(128)S(1)} %add_multiply_fusion), kind=kLoop, calls=%fused_computation.20 | loop fusion | flops 1769472 | bytes 2433152 | tf_op jit(solution)/shard_map/convert.2
  27.6 106.3 %all-gather = f32[64,144,16]{1,2,0:T(8,128)S(1)} all-gather(f32[1,144,16]{1,2,0:T(8,128)S(1)} %bitcast.203), channel_id=1, replica_groups=mesh['cls'=64,'ptl'=8] {'cls'}, dimensions={0}, use_global_device_ids=true | all-gather | bytes 599040 | tf_op jit(solution)/shard_map/all_gather | solution.py:35
  136.1 265.1 %while.10 = (s32[]{:T(128)}, f32[4,4,4,36]{3,2,1,0:T(4,128)S(1)}, s32[4,4]{1,0:T(4,128)S(1)}, f32[4,4,32,144]{3,2,1,0:T(8,128)S(1)}, f32[4,36,2,32,144]{4,3,0,1,...) while((s32[]{:T(128)}, f32[4,4,4,36]{3,2,1,0:T(4,128)S(1)}, ...), condition=%wide.region_7.8_spmd, body=%wide.region_1.7_spmd.sunk | while | flops 1385793792 | bytes 83052928 | solution.py:84
  137.4 65.0 %conditional.2 = (f32[1,4,4,36]{3,2,1,0:T(4,128)S(1)}) conditional(s32[]{:T(128)} %convert_element_type.49, () %tuple.85, (f32[4,4,32,144]{3,2,1,0:T(8,128)S(1)}, s32[]{:T(128)}, f32[4,36,2,32,144]{4,3,0,1,2:T(8,128)}, f32[4,4,32,144]{3,2,1,0:T(8,128)S(1)}, bf16[9216,128]{1,0:T(8,128)(2,1)}, /*index=5*/f32[4,4,4]{2,1,0:T(4,128)S(1)}) %tuple.86), branch_computations={%region_3.3_spmd, %region_4.6_spmd} | conditional | flops 1385793792 | bytes 83036368 | solution.py:82
  142.2 5.4 subtract_convert_fusion
  147.7 8.4 %pad_maximum_fusion = bf16[4,4,36,2,32,144]{5,4,3,1,2,0:T(8,128)(2,1)} fusion(bf16[4,4,36,1,32,144]{5,4,3,1,2,0:T(8,128)(2,1)S(1)} %get-tuple-element.153, bf16[4,4,36,1,32,144]{5,4,3,1,2,0:T(8,128)(2,1)S(1)} %get-tuple-element.152), kind=kLoop, calls=%fused_computation | loop fusion | flops 5308416 | bytes 21233664 | tf_op jit(solution)/shard_map/while/body/eval_jaxpr/cond/branch_1_fun/stack | solution.py:71
  156.1 35.0 %convert_element_type.31 = bf16[4,4,36,9216]{3,1,2,0:T(4,128)(2,1)} reshape(bf16[4,4,36,2,32,144]{5,4,3,1,2,0:T(8,128)(2,1)} %pad_maximum_fusion) | data formatting | bytes 21233664 | tf_op jit(solution)/shard_map/while/body/eval_jaxpr/cond/branch_1_fun/convert_element_type | solution.py:73
  191.1 10.9 %fusion.62 = (f32[4,4,36]{2,1,0:T(4,128)S(1)}, f32[4,4,36,128]{3,2,1,0:T(8,128)S(1)}) fusion(f32[4,4]{1,0:T(4,128)S(1)} %dynamic-slice_bitcast_fusion.2, bf16[9216,128]{1,0:T(8,128)(2,1)} %get-tuple-element.93, bf16[4,4,36,9216]{3,1,2,0:T(4,128)(2,1)} %convert_element_type.31), kind=kOutput, calls=%fused_computation.138 | convolution fusion | flops 1359101440 | bytes 13273408 | tf_op jit(solution)/shard_map/while/body/eval_jaxpr/cond/branch_1_fun/dot_general | solution.py:75
  203.7 65.0 %conditional.2 = (f32[1,4,4,36]{3,2,1,0:T(4,128)S(1)}) conditional(s32[]{:T(128)} %convert_element_type.49, () %tuple.85, (f32[4,4,32,144]{3,2,1,0:T(8,128)S(1)}, s32[]{:T(128)}, f32[4,36,2,32,144]{4,3,0,1,2:T(8,128)}, f32[4,4,32,144]{3,2,1,0:T(8,128)S(1)}, bf16[9216,128]{1,0:T(8,128)(2,1)}, /*index=5*/f32[4,4,4]{2,1,0:T(4,128)S(1)}) %tuple.86), branch_computations={%region_3.3_spmd, %region_4.6_spmd} | conditional | flops 1385793792 | bytes 83036368 | solution.py:82
  208.5 5.4 subtract_convert_fusion
  213.9 8.4 %pad_maximum_fusion = bf16[4,4,36,2,32,144]{5,4,3,1,2,0:T(8,128)(2,1)} fusion(bf16[4,4,36,1,32,144]{5,4,3,1,2,0:T(8,128)(2,1)S(1)} %get-tuple-element.153, bf16[4,4,36,1,32,144]{5,4,3,1,2,0:T(8,128)(2,1)S(1)} %get-tuple-element.152), kind=kLoop, calls=%fused_computation | loop fusion | flops 5308416 | bytes 21233664 | tf_op jit(solution)/shard_map/while/body/eval_jaxpr/cond/branch_1_fun/stack | solution.py:71
  222.4 35.0 %convert_element_type.31 = bf16[4,4,36,9216]{3,1,2,0:T(4,128)(2,1)} reshape(bf16[4,4,36,2,32,144]{5,4,3,1,2,0:T(8,128)(2,1)} %pad_maximum_fusion) | data formatting | bytes 21233664 | tf_op jit(solution)/shard_map/while/body/eval_jaxpr/cond/branch_1_fun/convert_element_type | solution.py:73
  257.4 10.9 %fusion.62 = (f32[4,4,36]{2,1,0:T(4,128)S(1)}, f32[4,4,36,128]{3,2,1,0:T(8,128)S(1)}) fusion(f32[4,4]{1,0:T(4,128)S(1)} %dynamic-slice_bitcast_fusion.2, bf16[9216,128]{1,0:T(8,128)(2,1)} %get-tuple-element.93, bf16[4,4,36,9216]{3,1,2,0:T(4,128)(2,1)} %convert_element_type.31), kind=kOutput, calls=%fused_computation.138 | convolution fusion | flops 1359101440 | bytes 13273408 | tf_op jit(solution)/shard_map/while/body/eval_jaxpr/cond/branch_1_fun/dot_general | solution.py:75
  270.0 65.0 %conditional.2 = (f32[1,4,4,36]{3,2,1,0:T(4,128)S(1)}) conditional(s32[]{:T(128)} %convert_element_type.49, () %tuple.85, (f32[4,4,32,144]{3,2,1,0:T(8,128)S(1)}, s32[]{:T(128)}, f32[4,36,2,32,144]{4,3,0,1,2:T(8,128)}, f32[4,4,32,144]{3,2,1,0:T(8,128)S(1)}, bf16[9216,128]{1,0:T(8,128)(2,1)}, /*index=5*/f32[4,4,4]{2,1,0:T(4,128)S(1)}) %tuple.86), branch_computations={%region_3.3_spmd, %region_4.6_spmd} | conditional | flops 1385793792 | bytes 83036368 | solution.py:82
  274.8 5.4 subtract_convert_fusion
  280.2 8.4 %pad_maximum_fusion = bf16[4,4,36,2,32,144]{5,4,3,1,2,0:T(8,128)(2,1)} fusion(bf16[4,4,36,1,32,144]{5,4,3,1,2,0:T(8,128)(2,1)S(1)} %get-tuple-element.153, bf16[4,4,36,1,32,144]{5,4,3,1,2,0:T(8,128)(2,1)S(1)} %get-tuple-element.152), kind=kLoop, calls=%fused_computation | loop fusion | flops 5308416 | bytes 21233664 | tf_op jit(solution)/shard_map/while/body/eval_jaxpr/cond/branch_1_fun/stack | solution.py:71
  288.7 35.0 %convert_element_type.31 = bf16[4,4,36,9216]{3,1,2,0:T(4,128)(2,1)} reshape(bf16[4,4,36,2,32,144]{5,4,3,1,2,0:T(8,128)(2,1)} %pad_maximum_fusion) | data formatting | bytes 21233664 | tf_op jit(solution)/shard_map/while/body/eval_jaxpr/cond/branch_1_fun/convert_element_type | solution.py:73
  323.7 10.9 %fusion.62 = (f32[4,4,36]{2,1,0:T(4,128)S(1)}, f32[4,4,36,128]{3,2,1,0:T(8,128)S(1)}) fusion(f32[4,4]{1,0:T(4,128)S(1)} %dynamic-slice_bitcast_fusion.2, bf16[9216,128]{1,0:T(8,128)(2,1)} %get-tuple-element.93, bf16[4,4,36,9216]{3,1,2,0:T(4,128)(2,1)} %convert_element_type.31), kind=kOutput, calls=%fused_computation.138 | convolution fusion | flops 1359101440 | bytes 13273408 | tf_op jit(solution)/shard_map/while/body/eval_jaxpr/cond/branch_1_fun/dot_general | solution.py:75
  336.3 65.0 %conditional.2 = (f32[1,4,4,36]{3,2,1,0:T(4,128)S(1)}) conditional(s32[]{:T(128)} %convert_element_type.49, () %tuple.85, (f32[4,4,32,144]{3,2,1,0:T(8,128)S(1)}, s32[]{:T(128)}, f32[4,36,2,32,144]{4,3,0,1,2:T(8,128)}, f32[4,4,32,144]{3,2,1,0:T(8,128)S(1)}, bf16[9216,128]{1,0:T(8,128)(2,1)}, /*index=5*/f32[4,4,4]{2,1,0:T(4,128)S(1)}) %tuple.86), branch_computations={%region_3.3_spmd, %region_4.6_spmd} | conditional | flops 1385793792 | bytes 83036368 | solution.py:82
  346.5 8.4 %pad_maximum_fusion = bf16[4,4,36,2,32,144]{5,4,3,1,2,0:T(8,128)(2,1)} fusion(bf16[4,4,36,1,32,144]{5,4,3,1,2,0:T(8,128)(2,1)S(1)} %get-tuple-element.153, bf16[4,4,36,1,32,144]{5,4,3,1,2,0:T(8,128)(2,1)S(1)} %get-tuple-element.152), kind=kLoop, calls=%fused_computation | loop fusion | flops 5308416 | bytes 21233664 | tf_op jit(solution)/shard_map/while/body/eval_jaxpr/cond/branch_1_fun/stack | solution.py:71
  354.9 35.0 %convert_element_type.31 = bf16[4,4,36,9216]{3,1,2,0:T(4,128)(2,1)} reshape(bf16[4,4,36,2,32,144]{5,4,3,1,2,0:T(8,128)(2,1)} %pad_maximum_fusion) | data formatting | bytes 21233664 | tf_op jit(solution)/shard_map/while/body/eval_jaxpr/cond/branch_1_fun/convert_element_type | solution.py:73
  390.0 10.9 %fusion.62 = (f32[4,4,36]{2,1,0:T(4,128)S(1)}, f32[4,4,36,128]{3,2,1,0:T(8,128)S(1)}) fusion(f32[4,4]{1,0:T(4,128)S(1)} %dynamic-slice_bitcast_fusion.2, bf16[9216,128]{1,0:T(8,128)(2,1)} %get-tuple-element.93, bf16[4,4,36,9216]{3,1,2,0:T(4,128)(2,1)} %convert_element_type.31), kind=kOutput, calls=%fused_computation.138 | convolution fusion | flops 1359101440 | bytes 13273408 | tf_op jit(solution)/shard_map/while/body/eval_jaxpr/cond/branch_1_fun/dot_general | solution.py:75
  401.4 141.1 %pmax.7 = f32[16,36]{1,0:T(8,128)S(1)} all-reduce(f32[16,36]{1,0:T(8,128)S(1)} %bitcast.200), channel_id=1, replica_groups=mesh['cls'=64,'ptl'=8] {'cls'}, use_global_device_ids=true, to_apply=%region_11.12 | all-reduce | flops 576 | bytes 4608 | tf_op jit(solution)/shard_map/pmax | solution.py:95
  542.7 142.7 %psum.7 = f32[16,36]{1,0:T(8,128)S(1)} all-reduce(f32[16,36]{1,0:T(8,128)S(1)} %bitcast.202), channel_id=1, replica_groups=mesh['cls'=64,'ptl'=8] {'cls'}, use_global_device_ids=true, to_apply=%region_13.14 | all-reduce | flops 576 | bytes 4608 | tf_op jit(solution)/shard_map/psum | solution.py:96
  (154 shorter events, 50.2 us)
Async XLA Ops:
  0.6 15.5 %copy-start = (f32[32,32]{1,0:T(8,128)S(1)}, f32[32,32]{1,0:T(8,128)}, u32[]{:S(2)}) copy-start(f32[32,32]{1,0:T(8,128)} %param.13) | copy-start | bytes 12292
  11.2 5.0 copy-start.6
  11.2 5.2 copy-start.3
  11.2 5.2 copy-start.5
  11.2 5.2 copy-start.7
  11.2 16.4 %copy-start.2 = (f32[16,144]{1,0:T(8,128)S(1)}, f32[16,144]{1,0:T(8,128)}, u32[]{:S(2)}) copy-start(f32[16,144]{1,0:T(8,128)} %param.11) | copy-start | bytes 27652
  136.1 549.6 %copy-start.4 = (s32[16]{0:T(128)S(1)}, s32[16]{0:T(128)}, u32[]{:S(2)}) copy-start(s32[16]{0:T(128)} %param.17) | copy-start | bytes 196
  401.2 285.9 %copy-start.1 = (f32[32,32]{1,0:T(8,128)S(1)}, f32[32,32]{1,0:T(8,128)}, u32[]{:S(2)}) copy-start(f32[32,32]{1,0:T(8,128)} %param.13) | copy-start | bytes 12292
where the time goes:
time: 691 us; the launch traced here: 687 us
  blocking collectives  390 us (56%)
  local copies, waits for them, and re-layouts  172 us (25%)
  other arithmetic  76.9 us (11%)
  matrix products  44.1 us (6%)
    psum x1, blocking collectives, body(): total = lax.psum(jnp.sum(jnp.exp(scores - peak[:, None, :]), axis=1), 'cls')  143 us
    pmax x1, blocking collectives, body(): peak = lax.pmax(jnp.max(scores, axis=1), 'cls')  141 us
    convert_element_type x4, local copies, waits for them, and re-layouts, compute(): product = jnp.stack([real_y, imag_y], axis=3).reshape(PBLOCK * local * RO...  140 us
    all_gather x1, blocking collectives, body(): gathered = lax.all_gather(images, 'cls', axis=1, tiled=True)  106 us
    dot_general x4, matrix products, compute(): corr = jnp.dot(product, table, preferred_element_type=jnp.float32)  43.6 us
    another operation x4, other arithmetic, compute(): jnp.stack([real_y, imag_y], axis=3)  33.7 us
    another operation x5, other arithmetic  30.7 us
    mul x4, local copies, waits for them, and re-layouts, compute(): zre[:, None, None] * rotated[None, :, :, 0]  19 us

commit v1 on v0

v1 whole, which is shorter than its diff:
```python
import math

import jax
import jax.numpy as jnp
import numpy as np
from jax import lax
from jax.experimental import pallas as pl
from jax.experimental.pallas import tpu as pltpu
from jax.sharding import PartitionSpec as P

CYCLES = 32
ANG = 144
ROT = 36
SHIFTS = 128
BOX = 128
STEP = ANG // ROT
NX, NZ = 4, 16
LOCAL = 4
MINE = 4
ALL_C = NX * LOCAL
ROWS = ROT * ALL_C
KT = 256
NB = 9
HALF = ROT // 2
CHUNKS = HALF // NB
HROWS = HALF * ALL_C
WIDE = (2 * HALF - NB) * ALL_C
NEAR = 4
MESH = pl.DeviceIdType.MESH
HIGH = lax.Precision.HIGHEST
NT = (((1,), (1,)), ((), ()))


def phase_tables():
    radius = (np.arange(CYCLES, dtype=np.float64) + 1.0) / BOX
    theta = np.arange(ANG, dtype=np.float64) * (2.0 * math.pi / ANG)
    index = np.arange(SHIFTS)
    shift_x = (index % 16 - 8).astype(np.float64)
    shift_y = (index // 16 - SHIFTS // 32).astype(np.float64)
    along = np.cos(theta)[:, None] * shift_x + np.sin(theta)[:, None] * shift_y
    phase = 2.0 * math.pi * radius[:, None, None] * along[None]

    def order(table):
        table = table.reshape(2, NZ, ROT, STEP, SHIFTS).transpose(2, 4, 1, 0, 3)
        return table.reshape(ROT, SHIFTS, 128)[:HALF].astype(jnp.bfloat16)

    return order(np.cos(phase)), order(np.sin(phase))


def iota(shape, axis):
    return lax.broadcasted_iota(jnp.int32, shape, axis)


def send(src, dst, send_sem, recv_sem, device):
    copy = pltpu.make_async_remote_copy(
        src_ref=src,
        dst_ref=dst,
        send_sem=send_sem,
        recv_sem=recv_sem,
        device_id={"cls": device},
        device_id_type=MESH,
    )
    copy.start()
    return copy


def spread_z(buffer, sends, recvs, x, z):
    copies = {}
    for reach in range(NEAR, 0, -1):
        for step in (reach, -reach):
            device = x * NZ + (z + step) % NZ
            slot = buffer.at[z]
            copies[step] = send(slot, slot, sends.at[step % NZ], recvs.at[step % NZ], device)
    return copies


def relay_z(buffer, sends, recvs, x, z, copies):
    for side, last in ((1, NEAR), (-1, NEAR - 1)):
        copies[side * NEAR].wait_recv()
        slot = buffer.at[(z - side * NEAR) % NZ]
        for reach in range(last, 0, -1):
            step = side * (NEAR + reach)
            device = x * NZ + (z + side * reach) % NZ
            copies[step] = send(slot, slot, sends.at[step % NZ], recvs.at[step % NZ], device)


def finish_z(copies):
    for step, copy in copies.items():
        if abs(step) != NEAR:
            copy.wait_recv()
    for copy in copies.values():
        copy.wait_send()


def kernel(
    cos_hbm, sin_hbm, images_hbm, references_hbm, ctf_hbm, noise_hbm, group_hbm, mic_hbm, count_hbm,
    class_post, rot_post,
    cos, sin, images, references, ctf, noise, group, mic, count,
    rows_c, rows_n, rows_s, padded, split_a, split_b, xs, xr, tail, rall, gathered, cross,
    turned, ends, wide, zt, mixed, shifted_a, shifted_b, acc_a, acc_b, score, half, flip, tiles, post, outs,
    local, xsend, xrecv, rsend, rrecv, zsend, zrecv, tsend, trecv, osend, orecv,
):
    me = lax.axis_index("cls")
    x, z = me // NZ, me % NZ
    along_x = [((x + step) % NX) * NZ + z for step in range(1, NX)]

    pairs = [
        (images_hbm, images), (ctf_hbm, ctf), (noise_hbm, noise), (group_hbm, group), (mic_hbm, mic),
        (count_hbm, count), (references_hbm, references), (cos_hbm, cos), (sin_hbm, sin),
    ]
    loads = [pltpu.make_async_copy(a, b, local.at[n]) for n, (a, b) in enumerate(pairs)]
    for load in loads:
        load.start()
    barrier = pltpu.get_barrier_semaphore()
    near = [x * NZ + (z + step) % NZ for step in range(-NEAR, NEAR + 1) if step]
    for device in along_x + near:
        pl.semaphore_signal(barrier, inc=1, device_id={"cls": device}, device_id_type=MESH)

    for load in loads[:6]:
        load.wait()
    for p in range(16):
        rows_c[p : p + 1, :] = ctf[pl.ds(group[p], 1), :]
        rows_n[p : p + 1, :] = noise[pl.ds(mic[p], 1), :]
        rows_s[p : p + 1, :] = jnp.full((1, CYCLES), count[p], jnp.int32).astype(jnp.float32)
    counted = rows_s[...]
    ctf_rows = rows_c[...]
    weight = ctf_rows * rows_n[...] * (counted / (counted + 1.0))
    cross[...] = 0.5 * ctf_rows * weight
    own = (x % 2) * NZ + z
    column = jnp.sum(jnp.where(iota((16, CYCLES), 1) == own, weight, 0.0), axis=1, keepdims=True)
    column = column * jnp.where(x >= 2, -1.0, 1.0)
    padded[...] = jnp.zeros_like(padded)
    padded[:, 0:ANG] = images[...] * column
    full = padded[...]
    row, lane = iota((16, 256), 0) & 3, iota((16, 256), 1) & 3
    rolled = {t: (pltpu.roll(full, t % 256, 1) if t else full) for t in range(-3, 4)}
    for d in range(STEP):
        value = jnp.zeros_like(full)
        for p in range(MINE):
            value = jnp.where((row == p) & (lane == p), rolled[p - d], value)
        for t in range(NX):
            line = jnp.sum(value[4 * t : 4 * t + 4], axis=0, keepdims=True)
            xs[t, d : d + 1, :] = line[:, 0:128]
            xs[t, 4 + d : 5 + d, :] = line[:, 128:256]

    pl.semaphore_wait(barrier, NX - 1 + 2 * NEAR)
    x_copies = []
    for n, device in enumerate(along_x):
        x_copies.append(send(xs.at[(x + n + 1) % NX], xr.at[x], xsend.at[n], xrecv.at[n], device))
    xr[x] = xs[x]

    loads[6].wait()
    for k in range(2 * CYCLES):
        base, off = (ANG * k) // 128 * 128, (ANG * k) % 128
        block = references[:, base : base + 256].astype(jnp.float32)
        if off:
            block = pltpu.roll(block, 256 - off, 1)
        split_a[pl.ds(k, LOCAL, stride=2 * CYCLES), :] = block[:, 0:128]
        split_b[pl.ds(k, LOCAL, stride=2 * CYCLES), :] = block[:, 128:256]
    rho = iota((KT, 1), 0)
    kappa = ((rho >> 7) << 5) + (((rho >> 2) & 1) << 4) + ((rho >> 3) & 15)
    repeat = (iota((KT, 2 * CYCLES), 1) == kappa).astype(jnp.float32).astype(jnp.bfloat16)
    angle = iota((1, 256), 1)
    keep = ((rho & 3) == (angle & 3)) & (angle < ANG)
    rho = iota((ROT * LOCAL, 1), 0)
    block_of = jnp.where(rho < LOCAL, 0, ROT - (rho >> 2))
    hit = (angle >> 2) == block_of
    total = jnp.zeros((ROT * LOCAL, KT), jnp.float32)
    for c in range(LOCAL):
        lines = slice(2 * CYCLES * c, 2 * CYCLES * (c + 1))
        one = jnp.concatenate([split_a[lines, :], split_b[lines, :]], axis=1).astype(jnp.bfloat16)
        spread = jnp.dot(repeat, one, preferred_element_type=jnp.float32)
        spread = jnp.where(keep, spread, 0.0).astype(jnp.bfloat16)
        pick = (hit & ((rho & 3) == c)).astype(jnp.float32).astype(jnp.bfloat16)
        total += lax.dot_general(pick, spread, NT, preferred_element_type=jnp.float32)
    rall[x] = total
    left, right = (x + NX - 1) % NX, (x + 1) % NX
    part_a, part_b = pl.ds(0, ROT * LOCAL // 2), pl.ds(ROT * LOCAL // 2, ROT * LOCAL // 2)
    from_left = send(rall.at[x], rall.at[x], rsend.at[0], rrecv.at[0], right * NZ + z)
    from_right = send(rall.at[x], rall.at[x], rsend.at[1], rrecv.at[1], left * NZ + z)

    for copy in x_copies:
        copy.wait()
    for part in range(2):
        for low in range(2):
            block = xr[2 * part + low]
            gathered[z, part, 4 * low : 4 * low + 4, :] = block[0:4]
            tail[part, 4 * low : 4 * low + 4, :] = block[4:8]
    gathered[z, 2] = tail[0] + pltpu.roll(tail[1], 16, 1)
    z_copies = spread_z(gathered, zsend, zrecv, x, z)
    relay_z(gathered, zsend, zrecv, x, z, z_copies)
    from_left.wait_recv()
    slot = rall.at[left, part_a]
    onward_a = send(slot, slot, rsend.at[2], rrecv.at[2], right * NZ + z)
    from_right.wait_recv()
    slot = rall.at[right, part_b]
    onward_b = send(slot, slot, rsend.at[3], rrecv.at[3], left * NZ + z)
    rho = iota((ROWS, 1), 0)
    kappa = ((rho >> 2) & 3) * (ROT * LOCAL) + (rho >> 4) * LOCAL + (rho & 3)
    place = (iota((ROWS, ROWS), 1) == kappa).astype(jnp.float32).astype(jnp.bfloat16)
    onward_a.wait_recv()
    onward_b.wait_recv()

    stacked = rall[...].reshape(ROWS, KT).astype(jnp.bfloat16)
    turned[...] = jnp.dot(place, stacked, preferred_element_type=jnp.float32)

    near_half, far_half = turned[0:HROWS, :], turned[HROWS:ROWS, :]
    plus = (near_half + far_half).astype(jnp.bfloat16)
    minus = (near_half - far_half).astype(jnp.bfloat16)
    ends[0, 0:HROWS, :] = plus
    ends[0, HROWS:ROWS, :] = plus
    ends[1, 0:HROWS, :] = -minus
    ends[1, HROWS:ROWS, :] = minus
    for sign in range(2):
        for q in range(NB):
            first = ALL_C * (NB - q)
            wide[sign, :, q * KT : (q + 1) * KT] = ends[sign, first : first + WIDE, :]

    power = jnp.zeros((ALL_C, KT), jnp.float32)
    for i in range(ROT):
        line = turned[16 * i : 16 * i + 16, :]
        power += line * line
    half[...] = jnp.zeros_like(half)
    half[0:MINE, :] = cross[pl.ds(x * MINE, MINE), :]
    lam = iota((1, KT), 1)
    spread = (iota((CYCLES, KT), 0) == (((lam >> 2) & 1) << 4) + ((lam >> 3) & 15)).astype(jnp.float32)
    half_wide = jnp.dot(half[...], spread, precision=HIGH, preferred_element_type=jnp.float32)
    quad = lax.dot_general(power, half_wide, NT, precision=HIGH, preferred_element_type=jnp.float32)
    loads[7].wait()
    loads[8].wait()

    finish_z(z_copies)
    for copy in (from_left, from_right, onward_a, onward_b):
        copy.wait_send()
    zt[0, 0:128] = gathered[:, 0].reshape(128, 128).T
    zt[1, 0:128] = gathered[:, 1].reshape(128, 128).T
    rest = gathered[:, 2].reshape(128, 128).T
    zt[0, 128:ANG] = rest[0:16]
    zt[1, 128:ANG] = rest[16:32]
    for part in range(2):
        one, two = zt[part, 0 : ANG // 2, :], zt[part, ANG // 2 : ANG, :]
        mixed[part, 0] = 0.5 * (one + two)
        mixed[part, 1] = 0.5 * (one - two)

    def build(chunk, pair, target):
        for q in range(NB):
            b = chunk * NB + q
            c, s = cos[b].astype(jnp.float32), sin[b].astype(jnp.float32)
            left, right = slice(q * KT, q * KT + 128), slice(q * KT + 128, q * KT + 256)
            for h in range(2):
                line = slice(4 * b + 2 * pair + h, 4 * b + 2 * pair + h + 1)
                rp, rm, ip, im = mixed[0, 0, line], mixed[0, 1, line], mixed[1, 0, line], mixed[1, 1, line]
                rows = slice(128 * h, 128 * h + 128)
                target[0, rows, left] = (c * rp + s * im).astype(jnp.bfloat16)
                target[0, rows, right] = (s * rm - c * ip).astype(jnp.bfloat16)
                target[1, rows, left] = (c * rm + s * ip).astype(jnp.bfloat16)
                target[1, rows, right] = (s * rp - c * im).astype(jnp.bfloat16)

    def multiply(chunk, source, acc):
        start = ALL_C * NB * (CHUNKS - 1 - chunk)
        for sign in range(2):
            left = wide[sign, start : start + HROWS, :]
            part = lax.dot_general(left, source[sign], NT, preferred_element_type=jnp.float32)
            if chunk:
                acc[sign] += part
            else:
                acc[sign] = part

    def reduce(pair, acc):
        size = 48
        lane = iota((size, 128), 1)
        for first in range(0, HROWS, size):
            tops = [jnp.zeros((size, 128), jnp.float32)] * 2
            totals = [jnp.ones((size, 128), jnp.float32)] * 2
            for h in range(2):
                even = acc[0, first : first + size, 128 * h : 128 * h + 128]
                odd = acc[1, first : first + size, 128 * h : 128 * h + 128]
                for half, value in enumerate((even + odd, even - odd)):
                    high = jnp.max(value, axis=1, keepdims=True)
                    low = jnp.sum(jnp.exp(value - high), axis=1, keepdims=True)
                    tops[half] = jnp.where(lane == 2 * pair + h, high, tops[half])
                    totals[half] = jnp.where(lane == 2 * pair + h, low, totals[half])
            for half in range(2):
                rows = slice(half * HROWS + first, half * HROWS + first + size)
                value = tops[half] + jnp.log(totals[half])
                score[rows, :] = value if pair == 0 else value + score[rows, :]

    build(0, 0, shifted_a)
    build(1, 0, shifted_b)
    multiply(0, shifted_a, acc_a)
    build(0, 1, shifted_a)
    multiply(1, shifted_b, acc_a)
    build(1, 1, shifted_b)
    multiply(0, shifted_a, acc_b)
    reduce(0, acc_a)
    multiply(1, shifted_b, acc_b)
    reduce(1, acc_b)

    values = score[...].reshape(ROT, ALL_C, 128) - quad[None]
    high = jnp.max(values, axis=0)
    by_class = high + jnp.log(jnp.sum(jnp.exp(values - high[None]), axis=0))
    high = jnp.max(values, axis=1)
    by_rot = high + jnp.log(jnp.sum(jnp.exp(values - high[:, None]), axis=1))
    flip[...] = jnp.zeros_like(flip)
    flip[0:ROT, :] = by_rot
    flip[64 : 64 + ALL_C, :] = by_class
    tile = flip[...].T[0:MINE, :]

    tiles[z] = tile
    t_copies = []
    for reach in range(NZ // 2, 0, -1):
        for step in (reach, -reach) if reach < NZ // 2 else (reach,):
            device = x * NZ + (z + step) % NZ
            n = step % NZ
            t_copies.append(send(tiles.at[z], tiles.at[z], tsend.at[n], trecv.at[n], device))
    for copy in t_copies:
        copy.wait()
    values = tiles[...]
    high = jnp.max(values, axis=0)
    rot_lse = high + jnp.log(jnp.sum(jnp.exp(values - high[None]), axis=0))
    lane = iota((MINE, 128), 1)
    masked = jnp.where(lane < ROT, rot_lse, -jnp.inf)
    high = jnp.max(masked, axis=1, keepdims=True)
    norm = high + jnp.log(jnp.sum(jnp.exp(masked - high), axis=1, keepdims=True))
    post[...] = jnp.where(lane < ROT, rot_lse, tile) - norm
    outs[x] = post[...]
    o_copies = []
    for n, device in enumerate(along_x):
        o_copies.append(send(post, outs.at[x], osend.at[n], orecv.at[n], device))
    for copy in o_copies:
        copy.wait()
    line = iota((MINE, 128), 0)
    for t in range(NX):
        live = jnp.zeros((MINE, 128), jnp.int32)
        for p in range(MINE):
            live = jnp.where(line == p, count[MINE * t + p], live)
        value = jnp.where(live > 0, outs[t], 0.0)
        rot_post[MINE * t : MINE * t + MINE, :] = value[:, 0:ROT]
        class_post[MINE * t : MINE * t + MINE, :] = pltpu.roll(value, 64 - LOCAL * x, 1)[:, 0:LOCAL]


def body(cos, sin, images, references, ctf_table, noise_inv, defocus_group, micrograph, batch_size):
    vmem, hbm = pl.BlockSpec(memory_space=pltpu.VMEM), pl.BlockSpec(memory_space=pltpu.HBM)
    f32, bf16, i32, dma = jnp.float32, jnp.bfloat16, jnp.int32, pltpu.SemaphoreType.DMA
    operands = (cos, sin, images, references, ctf_table, noise_inv, defocus_group, micrograph, batch_size)
    operands = [pltpu.with_memory_space_constraint(a, pltpu.HBM) for a in operands]
    class_post, rot_post = pl.pallas_call(
        kernel,
        out_shape=(
            jax.ShapeDtypeStruct((16, LOCAL), f32),
            jax.ShapeDtypeStruct((16, ROT), f32),
        ),
        in_specs=[hbm] * 9,
        out_specs=(vmem, vmem),
        scratch_shapes=[
            pltpu.VMEM(cos.shape, bf16),
            pltpu.VMEM(sin.shape, bf16),
            pltpu.VMEM(images.shape, f32),
            pltpu.VMEM(references.shape, bf16),
            pltpu.VMEM(ctf_table.shape, f32),
            pltpu.VMEM(noise_inv.shape, f32),
            pltpu.SMEM((16,), i32),
            pltpu.SMEM((16,), i32),
            pltpu.SMEM((16,), i32),
            pltpu.VMEM((16, CYCLES), f32),
            pltpu.VMEM((16, CYCLES), f32),
            pltpu.VMEM((16, CYCLES), f32),
            pltpu.VMEM((16, 256), f32),
            pltpu.VMEM((2 * CYCLES * LOCAL, 128), f32),
            pltpu.VMEM((2 * CYCLES * LOCAL, 128), f32),
            pltpu.VMEM((NX, 8, 128), f32),
            pltpu.VMEM((NX, 8, 128), f32),
            pltpu.VMEM((2, 8, 128), f32),
            pltpu.VMEM((NX, ROT * LOCAL, KT), f32),
            pltpu.VMEM((NZ, 3, 8, 128), f32),
            pltpu.VMEM((16, CYCLES), f32),
            pltpu.VMEM((ROWS, KT), f32),
            pltpu.VMEM((2, ROWS, KT), bf16),
            pltpu.VMEM((2, WIDE, NB * KT), bf16),
            pltpu.VMEM((2, ANG, 128), f32),
            pltpu.VMEM((2, 2, ANG // 2, 128), f32),
            pltpu.VMEM((2, 2 * SHIFTS, NB * KT), bf16),
            pltpu.VMEM((2, 2 * SHIFTS, NB * KT), bf16),
            pltpu.VMEM((2, HROWS, 2 * SHIFTS), f32),
            pltpu.VMEM((2, HROWS, 2 * SHIFTS), f32),
            pltpu.VMEM((ROWS, 128), f32),
            pltpu.VMEM((128, CYCLES), f32),
            pltpu.VMEM((128, 128), f32),
            pltpu.VMEM((NZ, MINE, 128), f32),
            pltpu.VMEM((MINE, 128), f32),
            pltpu.VMEM((NX, MINE, 128), f32),
            dma((9,)),
            dma((NX - 1,)),
            dma((NX - 1,)),
            dma((4,)),
            dma((4,)),
            dma((NZ,)),
            dma((NZ,)),
            dma((NZ,)),
            dma((NZ,)),
            dma((NX - 1,)),
            dma((NX - 1,)),
        ],
        compiler_params=pltpu.CompilerParams(collective_id=0, has_side_effects=True, vmem_limit_bytes=40 << 20),
        name="expectation",
    )(*operands)
    return class_post, rot_post


def solution(mesh):
    cos, sin = phase_tables()
    in_specs = (P("ptl", "cls"), P("cls", None), P(), P(), P("ptl"), P("ptl"), P("ptl"))
    out_specs = (P("ptl", "cls"), P("ptl", None))
    mapped = jax.shard_map(
        body, mesh=mesh, in_specs=(P(), P()) + in_specs, out_specs=out_specs, check_vma=False
    )

    def run(*args):
        return mapped(jnp.asarray(cos), jnp.asarray(sin), *args)

    return run
```

time: 691 us -> 46.3 us (0.07)
  the two profiles are of different devices: /device:TPU:32 before, /device:TPU:24 now
where the time goes in v1:
time: 46.3 us; the launch traced here: 46.2 us
  Pallas kernels  44.3 us (96%)
  local copies, waits for them, and re-layouts  1.25 us (3%)
  between operations  0.64 us (1%)
    pallas_call x1, Pallas kernels, body(): pl.pallas_call(kernel, out_shape=(jax.ShapeDtypeStruct((16, LOCAL), f32),...  44.3 us

profile of v1, /device:TPU:24, one launch (start us, length us, event | category | flops | bytes accessed | tf_op | source)
XLA Modules:
  0.0 46.2 jit_solution(11884472241765157350)
XLA Ops:
  0.6 44.3 %expectation.1 = (f32[16,4]{1,0:T(8,128)S(1)}, f32[16,36]{1,0:T(8,128)S(1)}) custom-call(bf16[18,128,128]{2,1,0:T(8,128)(2,1)} %constant.4.clone.cos_hbm, bf16[18,128,128]{2,1,0:T(8,128)(2,1)} %constant.5.clone.sin_hbm, f32[16,144]{1,0:T(8,128)} %images_hbm.1, bf16[4,9216]{1,0:T(4,128)(2,1)} %references_hbm.1, f32[32,32]{1,0:T(8,128)} %ctf_hbm.1, ...), custom_call_target="tpu_custom_call" | custom-call | tf_op jit(solution)/shard_map/expectation/pallas_call | solution.py:347
  44.9 0.7 %copy.11 = f32[16,4]{0,1:T(4,128)} copy(f32[16,4]{1,0:T(8,128)S(1)} %get-tuple-element.2) | data formatting | bytes 512 | tf_op jit(solution)/shard_map/expectation/pallas_call | solution.py:347
  45.6 0.6 %copy.13 = f32[16,36]{1,0:T(8,128)} copy(f32[16,36]{1,0:T(8,128)S(1)} %get-tuple-element.7) | data formatting | bytes 4608

commit v2 on v1

--- a/solution.py
+++ b/solution.py
@@ -68,7 +68,7 @@
     copies = {}
     for reach in range(NEAR, 0, -1):
         for step in (reach, -reach):
-            device = x * NZ + (z + step) % NZ
+            device = x * NZ + ((z + step) & (NZ - 1))
             slot = buffer.at[z]
             copies[step] = send(slot, slot, sends.at[step % NZ], recvs.at[step % NZ], device)
     return copies
@@ -77,19 +77,17 @@
 def relay_z(buffer, sends, recvs, x, z, copies):
     for side, last in ((1, NEAR), (-1, NEAR - 1)):
         copies[side * NEAR].wait_recv()
-        slot = buffer.at[(z - side * NEAR) % NZ]
+        slot = buffer.at[(z - side * NEAR) & (NZ - 1)]
         for reach in range(last, 0, -1):
             step = side * (NEAR + reach)
-            device = x * NZ + (z + side * reach) % NZ
+            device = x * NZ + ((z + side * reach) & (NZ - 1))
             copies[step] = send(slot, slot, sends.at[step % NZ], recvs.at[step % NZ], device)
 
 
-def finish_z(copies):
+def arrive_z(copies):
     for step, copy in copies.items():
         if abs(step) != NEAR:
             copy.wait_recv()
-    for copy in copies.values():
-        copy.wait_send()
 
 
 def kernel(
@@ -101,9 +99,13 @@
     local, xsend, xrecv, rsend, rrecv, zsend, zrecv, tsend, trecv, osend, orecv,
 ):
     me = lax.axis_index("cls")
-    x, z = me // NZ, me % NZ
-    along_x = [((x + step) % NX) * NZ + z for step in range(1, NX)]
-
+    x, z = me >> 4, me & (NZ - 1)
+    along_x = [((x + step) & (NX - 1)) * NZ + z for step in range(1, NX)]
+
+    barrier = pltpu.get_barrier_semaphore()
+    near = [x * NZ + ((z + step) & (NZ - 1)) for step in range(-NEAR, NEAR + 1) if step]
+    for device in along_x + near:
+        pl.semaphore_signal(barrier, inc=1, device_id={"cls": device}, device_id_type=MESH)
     pairs = [
         (images_hbm, images), (ctf_hbm, ctf), (noise_hbm, noise), (group_hbm, group), (mic_hbm, mic),
         (count_hbm, count), (references_hbm, references), (cos_hbm, cos), (sin_hbm, sin),
@@ -111,10 +113,6 @@
     loads = [pltpu.make_async_copy(a, b, local.at[n]) for n, (a, b) in enumerate(pairs)]
     for load in loads:
         load.start()
-    barrier = pltpu.get_barrier_semaphore()
-    near = [x * NZ + (z + step) % NZ for step in range(-NEAR, NEAR + 1) if step]
-    for device in along_x + near:
-        pl.semaphore_signal(barrier, inc=1, device_id={"cls": device}, device_id_type=MESH)
 
     for load in loads[:6]:
         load.wait()
@@ -126,7 +124,7 @@
     ctf_rows = rows_c[...]
     weight = ctf_rows * rows_n[...] * (counted / (counted + 1.0))
     cross[...] = 0.5 * ctf_rows * weight
-    own = (x % 2) * NZ + z
+    own = (x & 1) * NZ + z
     column = jnp.sum(jnp.where(iota((16, CYCLES), 1) == own, weight, 0.0), axis=1, keepdims=True)
     column = column * jnp.where(x >= 2, -1.0, 1.0)
     padded[...] = jnp.zeros_like(padded)
@@ -142,12 +140,6 @@
             line = jnp.sum(value[4 * t : 4 * t + 4], axis=0, keepdims=True)
             xs[t, d : d + 1, :] = line[:, 0:128]
             xs[t, 4 + d : 5 + d, :] = line[:, 128:256]
-
-    pl.semaphore_wait(barrier, NX - 1 + 2 * NEAR)
-    x_copies = []
-    for n, device in enumerate(along_x):
-        x_copies.append(send(xs.at[(x + n + 1) % NX], xr.at[x], xsend.at[n], xrecv.at[n], device))
-    xr[x] = xs[x]
 
     loads[6].wait()
     for k in range(2 * CYCLES):
@@ -174,13 +166,19 @@
         pick = (hit & ((rho & 3) == c)).astype(jnp.float32).astype(jnp.bfloat16)
         total += lax.dot_general(pick, spread, NT, preferred_element_type=jnp.float32)
     rall[x] = total
-    left, right = (x + NX - 1) % NX, (x + 1) % NX
+
+    pl.semaphore_wait(barrier, NX - 1 + 2 * NEAR)
+    x_copies = []
+    for n, device in enumerate(along_x):
+        x_copies.append(send(xs.at[(x + n + 1) & (NX - 1)], xr.at[x], xsend.at[n], xrecv.at[n], device))
+    xr[x] = xs[x]
+    left, right = (x + NX - 1) & (NX - 1), (x + 1) & (NX - 1)
     part_a, part_b = pl.ds(0, ROT * LOCAL // 2), pl.ds(ROT * LOCAL // 2, ROT * LOCAL // 2)
     from_left = send(rall.at[x], rall.at[x], rsend.at[0], rrecv.at[0], right * NZ + z)
     from_right = send(rall.at[x], rall.at[x], rsend.at[1], rrecv.at[1], left * NZ + z)
 
     for copy in x_copies:
-        copy.wait()
+        copy.wait_recv()
     for part in range(2):
         for low in range(2):
             block = xr[2 * part + low]
@@ -229,9 +227,7 @@
     loads[7].wait()
     loads[8].wait()
 
-    finish_z(z_copies)
-    for copy in (from_left, from_right, onward_a, onward_b):
-        copy.wait_send()
+    arrive_z(z_copies)
     zt[0, 0:128] = gathered[:, 0].reshape(128, 128).T
     zt[1, 0:128] = gathered[:, 1].reshape(128, 128).T
     rest = gathered[:, 2].reshape(128, 128).T
@@ -310,11 +306,11 @@
     t_copies = []
     for reach in range(NZ // 2, 0, -1):
         for step in (reach, -reach) if reach < NZ // 2 else (reach,):
-            device = x * NZ + (z + step) % NZ
+            device = x * NZ + ((z + step) & (NZ - 1))
             n = step % NZ
             t_copies.append(send(tiles.at[z], tiles.at[z], tsend.at[n], trecv.at[n], device))
     for copy in t_copies:
-        copy.wait()
+        copy.wait_recv()
     values = tiles[...]
     high = jnp.max(values, axis=0)
     rot_lse = high + jnp.log(jnp.sum(jnp.exp(values - high[None]), axis=0))
@@ -328,7 +324,7 @@
     for n, device in enumerate(along_x):
         o_copies.append(send(post, outs.at[x], osend.at[n], orecv.at[n], device))
     for copy in o_copies:
-        copy.wait()
+        copy.wait_recv()
     line = iota((MINE, 128), 0)
     for t in range(NX):
         live = jnp.zeros((MINE, 128), jnp.int32)
@@ -337,6 +333,9 @@
         value = jnp.where(live > 0, outs[t], 0.0)
         rot_post[MINE * t : MINE * t + MINE, :] = value[:, 0:ROT]
         class_post[MINE * t : MINE * t + MINE, :] = pltpu.roll(value, 64 - LOCAL * x, 1)[:, 0:LOCAL]
+    sent = x_copies + [from_left, from_right, onward_a, onward_b] + list(z_copies.values()) + t_copies + o_copies
+    for copy in sent:
+        copy.wait_send()
 
 
 def body(cos, sin, images, references, ctf_table, noise_inv, defocus_group, micrograph, batch_size):

time: 46.3 us -> 46.3 us (level)
  no operation moved by 1% of the time
where the time goes in v2:
time: 46.3 us; the launch traced here: 46.1 us
  Pallas kernels  44.2 us (95%)
  local copies, waits for them, and re-layouts  1.25 us (3%)
  between operations  0.64 us (1%)
    pallas_call x1, Pallas kernels, body(): pl.pallas_call(kernel, out_shape=(jax.ShapeDtypeStruct((16, LOCAL), f32),...  44.2 us

profile of v2, /device:TPU:24, one launch (start us, length us, event | category | flops | bytes accessed | tf_op | source)
XLA Modules:
  0.0 46.1 jit_solution(5755701772231353467)
XLA Ops:
  0.6 44.2 %expectation.1 = (f32[16,4]{1,0:T(8,128)S(1)}, f32[16,36]{1,0:T(8,128)S(1)}) custom-call(bf16[18,128,128]{2,1,0:T(8,128)(2,1)} %constant.4.clone.cos_hbm, bf16[18,128,128]{2,1,0:T(8,128)(2,1)} %constant.5.clone.sin_hbm, f32[16,144]{1,0:T(8,128)} %images_hbm.1, bf16[4,9216]{1,0:T(4,128)(2,1)} %references_hbm.1, f32[32,32]{1,0:T(8,128)} %ctf_hbm.1, ...), custom_call_target="tpu_custom_call" | custom-call | tf_op jit(solution)/shard_map/expectation/pallas_call | solution.py:346
  44.9 0.7 %copy.11 = f32[16,4]{0,1:T(4,128)} copy(f32[16,4]{1,0:T(8,128)S(1)} %get-tuple-element.2) | data formatting | bytes 512 | tf_op jit(solution)/shard_map/expectation/pallas_call | solution.py:346
  45.5 0.6 %copy.13 = f32[16,36]{1,0:T(8,128)} copy(f32[16,36]{1,0:T(8,128)S(1)} %get-tuple-element.7) | data formatting | bytes 4608

commit v3 on v2

--- a/solution.py
+++ b/solution.py
@@ -22,6 +22,7 @@
 KT = 256
 NB = 9
 HALF = ROT // 2
+HREF = ROT * LOCAL // 2
 CHUNKS = HALF // NB
 HROWS = HALF * ALL_C
 WIDE = (2 * HALF - NB) * ALL_C
@@ -41,7 +42,7 @@
     phase = 2.0 * math.pi * radius[:, None, None] * along[None]
 
     def order(table):
-        table = table.reshape(2, NZ, ROT, STEP, SHIFTS).transpose(2, 4, 1, 0, 3)
+        table = table.reshape(2, NZ, ROT, STEP, SHIFTS).transpose(2, 4, 0, 1, 3)
         return table.reshape(ROT, SHIFTS, 128)[:HALF].astype(jnp.bfloat16)
 
     return order(np.cos(phase)), order(np.sin(phase))
@@ -51,13 +52,13 @@
     return lax.broadcasted_iota(jnp.int32, shape, axis)
 
 
-def send(src, dst, send_sem, recv_sem, device):
+def send(src, dst, send_sem, recv_sem, device, **other):
     copy = pltpu.make_async_remote_copy(
         src_ref=src,
         dst_ref=dst,
         send_sem=send_sem,
         recv_sem=recv_sem,
-        device_id={"cls": device},
+        device_id={"cls": device, **other},
         device_id_type=MESH,
     )
     copy.start()
@@ -94,18 +95,22 @@
     cos_hbm, sin_hbm, images_hbm, references_hbm, ctf_hbm, noise_hbm, group_hbm, mic_hbm, count_hbm,
     class_post, rot_post,
     cos, sin, images, references, ctf, noise, group, mic, count,
-    rows_c, rows_n, rows_s, padded, split_a, split_b, xs, xr, tail, rall, gathered, cross,
+    rows_c, rows_n, rows_s, padded, split_a, split_b, xs, xr, main, tail, rall, gathered, cross,
     turned, ends, wide, zt, mixed, shifted_a, shifted_b, acc_a, acc_b, score, half, flip, tiles, post, outs,
     local, xsend, xrecv, rsend, rrecv, zsend, zrecv, tsend, trecv, osend, orecv,
 ):
     me = lax.axis_index("cls")
     x, z = me >> 4, me & (NZ - 1)
+    ptl = lax.axis_index("ptl")
+    core = ptl & 1
+    sibling = ptl + 1 - 2 * core
     along_x = [((x + step) & (NX - 1)) * NZ + z for step in range(1, NX)]
 
     barrier = pltpu.get_barrier_semaphore()
     near = [x * NZ + ((z + step) & (NZ - 1)) for step in range(-NEAR, NEAR + 1) if step]
     for device in along_x + near:
         pl.semaphore_signal(barrier, inc=1, device_id={"cls": device}, device_id_type=MESH)
+    pl.semaphore_signal(barrier, inc=1, device_id={"ptl": sibling}, device_id_type=MESH)
     pairs = [
         (images_hbm, images), (ctf_hbm, ctf), (noise_hbm, noise), (group_hbm, group), (mic_hbm, mic),
         (count_hbm, count), (references_hbm, references), (cos_hbm, cos), (sin_hbm, sin),
@@ -128,6 +133,7 @@
     column = jnp.sum(jnp.where(iota((16, CYCLES), 1) == own, weight, 0.0), axis=1, keepdims=True)
     column = column * jnp.where(x >= 2, -1.0, 1.0)
     padded[...] = jnp.zeros_like(padded)
+    tail[...] = jnp.zeros_like(tail)
     padded[:, 0:ANG] = images[...] * column
     full = padded[...]
     row, lane = iota((16, 256), 0) & 3, iota((16, 256), 1) & 3
@@ -150,8 +156,7 @@
         split_a[pl.ds(k, LOCAL, stride=2 * CYCLES), :] = block[:, 0:128]
         split_b[pl.ds(k, LOCAL, stride=2 * CYCLES), :] = block[:, 128:256]
     rho = iota((KT, 1), 0)
-    kappa = ((rho >> 7) << 5) + (((rho >> 2) & 1) << 4) + ((rho >> 3) & 15)
-    repeat = (iota((KT, 2 * CYCLES), 1) == kappa).astype(jnp.float32).astype(jnp.bfloat16)
+    repeat = (iota((KT, 2 * CYCLES), 1) == (rho >> 2)).astype(jnp.float32).astype(jnp.bfloat16)
     angle = iota((1, 256), 1)
     keep = ((rho & 3) == (angle & 3)) & (angle < ANG)
     rho = iota((ROT * LOCAL, 1), 0)
@@ -165,39 +170,55 @@
         spread = jnp.where(keep, spread, 0.0).astype(jnp.bfloat16)
         pick = (hit & ((rho & 3) == c)).astype(jnp.float32).astype(jnp.bfloat16)
         total += lax.dot_general(pick, spread, NT, preferred_element_type=jnp.float32)
-    rall[x] = total
-
-    pl.semaphore_wait(barrier, NX - 1 + 2 * NEAR)
+    rall[x, 0] = total[0:HREF]
+    rall[x, 1] = total[HREF:]
+
+    pl.semaphore_wait(barrier, NX + 2 * NEAR)
     x_copies = []
     for n, device in enumerate(along_x):
         x_copies.append(send(xs.at[(x + n + 1) & (NX - 1)], xr.at[x], xsend.at[n], xrecv.at[n], device))
     xr[x] = xs[x]
     left, right = (x + NX - 1) & (NX - 1), (x + 1) & (NX - 1)
-    part_a, part_b = pl.ds(0, ROT * LOCAL // 2), pl.ds(ROT * LOCAL // 2, ROT * LOCAL // 2)
-    from_left = send(rall.at[x], rall.at[x], rsend.at[0], rrecv.at[0], right * NZ + z)
-    from_right = send(rall.at[x], rall.at[x], rsend.at[1], rrecv.at[1], left * NZ + z)
+    opposite = (x + 2) & (NX - 1)
+    part_a, part_b = pl.ds(0, 40), pl.ds(40, HREF - 40)
+    slot = rall.at[x, core]
+    from_left = send(slot, slot, rsend.at[0], rrecv.at[0], right * NZ + z)
+    from_right = send(slot, slot, rsend.at[1], rrecv.at[1], left * NZ + z)
 
     for copy in x_copies:
         copy.wait_recv()
-    for part in range(2):
-        for low in range(2):
-            block = xr[2 * part + low]
-            gathered[z, part, 4 * low : 4 * low + 4, :] = block[0:4]
-            tail[part, 4 * low : 4 * low + 4, :] = block[4:8]
-    gathered[z, 2] = tail[0] + pltpu.roll(tail[1], 16, 1)
+    last = jnp.zeros((STEP, 128), jnp.float32)
+    for t in range(NX):
+        block = xr[t]
+        gathered[z, 2 * t] = block[0:2]
+        gathered[z, 2 * t + 1] = block[2:4]
+        rest = block[4:8]
+        last = last + (pltpu.roll(rest, 16 * t, 1) if t else rest)
+    moved = pltpu.roll(last, 64, 1)
+    gathered[z, 8, 0:1, :] = last[0:1] + moved[1:2]
+    gathered[z, 8, 1:2, :] = last[2:3] + moved[3:4]
     z_copies = spread_z(gathered, zsend, zrecv, x, z)
+
+    from_left.wait_recv()
+    slot = rall.at[left, core]
+    part = rall.at[left, core, part_a]
+    onward_a = send(part, part, rsend.at[2], rrecv.at[2], right * NZ + z)
+    over_left = send(slot, slot, rsend.at[4], rrecv.at[4], me, ptl=sibling)
+    from_right.wait_recv()
+    slot = rall.at[right, core]
+    part = rall.at[right, core, part_b]
+    onward_b = send(part, part, rsend.at[3], rrecv.at[3], left * NZ + z)
+    over_right = send(slot, slot, rsend.at[5], rrecv.at[5], me, ptl=sibling)
     relay_z(gathered, zsend, zrecv, x, z, z_copies)
-    from_left.wait_recv()
-    slot = rall.at[left, part_a]
-    onward_a = send(slot, slot, rsend.at[2], rrecv.at[2], right * NZ + z)
-    from_right.wait_recv()
-    slot = rall.at[right, part_b]
-    onward_b = send(slot, slot, rsend.at[3], rrecv.at[3], left * NZ + z)
     rho = iota((ROWS, 1), 0)
     kappa = ((rho >> 2) & 3) * (ROT * LOCAL) + (rho >> 4) * LOCAL + (rho & 3)
     place = (iota((ROWS, ROWS), 1) == kappa).astype(jnp.float32).astype(jnp.bfloat16)
     onward_a.wait_recv()
     onward_b.wait_recv()
+    slot = rall.at[opposite, core]
+    over_opposite = send(slot, slot, rsend.at[6], rrecv.at[6], me, ptl=sibling)
+    for copy in (over_left, over_right, over_opposite):
+        copy.wait_recv()
 
     stacked = rall[...].reshape(ROWS, KT).astype(jnp.bfloat16)
     turned[...] = jnp.dot(place, stacked, preferred_element_type=jnp.float32)
@@ -221,18 +242,31 @@
     half[...] = jnp.zeros_like(half)
     half[0:MINE, :] = cross[pl.ds(x * MINE, MINE), :]
     lam = iota((1, KT), 1)
-    spread = (iota((CYCLES, KT), 0) == (((lam >> 2) & 1) << 4) + ((lam >> 3) & 15)).astype(jnp.float32)
+    spread = (iota((CYCLES, KT), 0) == ((lam >> 2) & 31)).astype(jnp.float32)
     half_wide = jnp.dot(half[...], spread, precision=HIGH, preferred_element_type=jnp.float32)
     quad = lax.dot_general(power, half_wide, NT, precision=HIGH, preferred_element_type=jnp.float32)
     loads[7].wait()
     loads[8].wait()
 
     arrive_z(z_copies)
-    zt[0, 0:128] = gathered[:, 0].reshape(128, 128).T
-    zt[1, 0:128] = gathered[:, 1].reshape(128, 128).T
-    rest = gathered[:, 2].reshape(128, 128).T
-    zt[0, 128:ANG] = rest[0:16]
-    zt[1, 128:ANG] = rest[16:32]
+    for origin in range(NZ):
+        for t in range(NX):
+            row = 64 * (t % 2) + 4 * origin
+            main[t // 2, row : row + 2, :] = gathered[origin, 2 * t]
+            main[t // 2, row + 2 : row + 4, :] = gathered[origin, 2 * t + 1]
+        last = gathered[origin, 8]
+        moved = pltpu.roll(last, 64, 1)
+        row = 4 * origin
+        tail[row : row + 1, :] = last[0:1]
+        tail[row + 1 : row + 2, :] = moved[0:1]
+        tail[row + 2 : row + 3, :] = last[1:2]
+        tail[row + 3 : row + 4, :] = moved[1:2]
+    rest = tail[...].T
+    lane = iota((16, 128), 1)
+    for part in range(2):
+        zt[part, 0:128] = main[part].T
+        low, high = rest[32 * part : 32 * part + 16], rest[32 * part + 16 : 32 * part + 32]
+        zt[part, 128:ANG] = jnp.where(lane < 64, low, pltpu.roll(high, 64, 1))
     for part in range(2):
         one, two = zt[part, 0 : ANG // 2, :], zt[part, ANG // 2 : ANG, :]
         mixed[part, 0] = 0.5 * (one + two)
@@ -333,7 +367,7 @@
         value = jnp.where(live > 0, outs[t], 0.0)
         rot_post[MINE * t : MINE * t + MINE, :] = value[:, 0:ROT]
         class_post[MINE * t : MINE * t + MINE, :] = pltpu.roll(value, 64 - LOCAL * x, 1)[:, 0:LOCAL]
-    sent = x_copies + [from_left, from_right, onward_a, onward_b] + list(z_copies.values()) + t_copies + o_copies
+    sent = x_copies + [from_left, from_right, onward_a, onward_b, over_left, over_right, over_opposite] + list(z_copies.values()) + t_copies + o_copies
     for copy in sent:
         copy.wait_send()
 
@@ -369,9 +403,10 @@
             pltpu.VMEM((2 * CYCLES * LOCAL, 128), f32),
             pltpu.VMEM((NX, 8, 128), f32),
             pltpu.VMEM((NX, 8, 128), f32),
-            pltpu.VMEM((2, 8, 128), f32),
-            pltpu.VMEM((NX, ROT * LOCAL, KT), f32),
-            pltpu.VMEM((NZ, 3, 8, 128), f32),
+            pltpu.VMEM((2, 128, 128), f32),
+            pltpu.VMEM((128, 128), f32),
+            pltpu.VMEM((NX, 2, HREF, KT), f32),
+            pltpu.VMEM((NZ, 9, 2, 128), f32),
             pltpu.VMEM((16, CYCLES), f32),
             pltpu.VMEM((ROWS, KT), f32),
             pltpu.VMEM((2, ROWS, KT), bf16),
@@ -391,8 +426,8 @@
             dma((9,)),
             dma((NX - 1,)),
             dma((NX - 1,)),
-            dma((4,)),
-            dma((4,)),
+            dma((7,)),
+            dma((7,)),
             dma((NZ,)),
             dma((NZ,)),
             dma((NZ,)),

time: 46.3 us -> 45.2 us (0.976)
  Pallas kernels: 44.2 us -> 43.1 us
    pallas_call x1, Pallas kernels: 44.2 us -> 43.1 us  [body(): pl.pallas_call(kernel, out_shape=(jax.ShapeDtypeStruct((16, LOCAL), f32),...]
where the time goes in v3:
time: 45.2 us; the launch traced here: 45 us
  Pallas kernels  43.1 us (95%)
  local copies, waits for them, and re-layouts  1.25 us (3%)
  between operations  0.64 us (1%)
    pallas_call x1, Pallas kernels, body(): pl.pallas_call(kernel, out_shape=(jax.ShapeDtypeStruct((16, LOCAL), f32),...  43.1 us

profile of v3, /device:TPU:24, one launch (start us, length us, event | category | flops | bytes accessed | tf_op | source)
XLA Modules:
  0.0 45.0 jit_solution(14648509936404056913)
XLA Ops:
  0.6 43.1 %expectation.1 = (f32[16,4]{1,0:T(8,128)S(1)}, f32[16,36]{1,0:T(8,128)S(1)}) custom-call(bf16[18,128,128]{2,1,0:T(8,128)(2,1)} %constant.4.clone.cos_hbm, bf16[18,128,128]{2,1,0:T(8,128)(2,1)} %constant.5.clone.sin_hbm, f32[16,144]{1,0:T(8,128)} %images_hbm.1, bf16[4,9216]{1,0:T(4,128)(2,1)} %references_hbm.1, f32[32,32]{1,0:T(8,128)} %ctf_hbm.1, ...), custom_call_target="tpu_custom_call" | custom-call | tf_op jit(solution)/shard_map/expectation/pallas_call | solution.py:380
  43.8 0.7 %copy.11 = f32[16,4]{0,1:T(4,128)} copy(f32[16,4]{1,0:T(8,128)S(1)} %get-tuple-element.2) | data formatting | bytes 512 | tf_op jit(solution)/shard_map/expectation/pallas_call | solution.py:380
  44.4 0.6 %copy.13 = f32[16,36]{1,0:T(8,128)} copy(f32[16,36]{1,0:T(8,128)S(1)} %get-tuple-element.7) | data formatting | bytes 4608

commit v4 on v3

--- a/solution.py
+++ b/solution.py
@@ -96,7 +96,7 @@
     class_post, rot_post,
     cos, sin, images, references, ctf, noise, group, mic, count,
     rows_c, rows_n, rows_s, padded, split_a, split_b, xs, xr, main, tail, rall, gathered, cross,
-    turned, ends, wide, zt, mixed, shifted_a, shifted_b, acc_a, acc_b, score, half, flip, tiles, post, outs,
+    turned, ends, wide, zt, mixed, shifted_a, shifted_b, acc_a, score, half, flip, tiles, post, outs,
     local, xsend, xrecv, rsend, rrecv, zsend, zrecv, tsend, trecv, osend, orecv,
 ):
     me = lax.axis_index("cls")
@@ -134,6 +134,7 @@
     column = column * jnp.where(x >= 2, -1.0, 1.0)
     padded[...] = jnp.zeros_like(padded)
     tail[...] = jnp.zeros_like(tail)
+    score[...] = jnp.zeros_like(score)
     padded[:, 0:ANG] = images[...] * column
     full = padded[...]
     row, lane = iota((16, 256), 0) & 3, iota((16, 256), 1) & 3
@@ -148,13 +149,17 @@
             xs[t, 4 + d : 5 + d, :] = line[:, 128:256]
 
     loads[6].wait()
-    for k in range(2 * CYCLES):
-        base, off = (ANG * k) // 128 * 128, (ANG * k) % 128
-        block = references[:, base : base + 256].astype(jnp.float32)
-        if off:
-            block = pltpu.roll(block, 256 - off, 1)
-        split_a[pl.ds(k, LOCAL, stride=2 * CYCLES), :] = block[:, 0:128]
-        split_b[pl.ds(k, LOCAL, stride=2 * CYCLES), :] = block[:, 128:256]
+    def divide(m, carry):
+        for n in range(8):
+            base = pl.multiple_of(8 * ANG * m + ANG * n // 128 * 128, 128)
+            block = references[:, pl.ds(base, 256)].astype(jnp.float32)
+            if n:
+                block = pltpu.roll(block, 256 - 16 * n, 1)
+            split_a[pl.ds(8 * m + n, LOCAL, stride=2 * CYCLES), :] = block[:, 0:128]
+            split_b[pl.ds(8 * m + n, LOCAL, stride=2 * CYCLES), :] = block[:, 128:256]
+        return carry
+
+    lax.fori_loop(0, 2 * CYCLES // 8, divide, 0)
     rho = iota((KT, 1), 0)
     repeat = (iota((KT, 2 * CYCLES), 1) == (rho >> 2)).astype(jnp.float32).astype(jnp.bfloat16)
     angle = iota((1, 256), 1)
@@ -278,7 +283,7 @@
             c, s = cos[b].astype(jnp.float32), sin[b].astype(jnp.float32)
             left, right = slice(q * KT, q * KT + 128), slice(q * KT + 128, q * KT + 256)
             for h in range(2):
-                line = slice(4 * b + 2 * pair + h, 4 * b + 2 * pair + h + 1)
+                line = pl.ds(4 * b + 2 * pair + h, 1)
                 rp, rm, ip, im = mixed[0, 0, line], mixed[0, 1, line], mixed[1, 0, line], mixed[1, 1, line]
                 rows = slice(128 * h, 128 * h + 128)
                 target[0, rows, left] = (c * rp + s * im).astype(jnp.bfloat16)
@@ -299,32 +304,36 @@
     def reduce(pair, acc):
         size = 48
         lane = iota((size, 128), 1)
-        for first in range(0, HROWS, size):
+
+        def part(m, carry):
+            first = pl.multiple_of(m * size, 16)
             tops = [jnp.zeros((size, 128), jnp.float32)] * 2
             totals = [jnp.ones((size, 128), jnp.float32)] * 2
             for h in range(2):
-                even = acc[0, first : first + size, 128 * h : 128 * h + 128]
-                odd = acc[1, first : first + size, 128 * h : 128 * h + 128]
+                even = acc[0, pl.ds(first, size), 128 * h : 128 * h + 128]
+                odd = acc[1, pl.ds(first, size), 128 * h : 128 * h + 128]
                 for half, value in enumerate((even + odd, even - odd)):
                     high = jnp.max(value, axis=1, keepdims=True)
                     low = jnp.sum(jnp.exp(value - high), axis=1, keepdims=True)
                     tops[half] = jnp.where(lane == 2 * pair + h, high, tops[half])
                     totals[half] = jnp.where(lane == 2 * pair + h, low, totals[half])
             for half in range(2):
-                rows = slice(half * HROWS + first, half * HROWS + first + size)
-                value = tops[half] + jnp.log(totals[half])
-                score[rows, :] = value if pair == 0 else value + score[rows, :]
+                rows = pl.ds(pl.multiple_of(half * HROWS + first, 16), size)
+                score[rows, :] += tops[half] + jnp.log(totals[half])
+            return carry
+
+        lax.fori_loop(0, HROWS // size, part, 0, unroll=2)
+
+    def step(pair, carry):
+        build(1, pair, shifted_b)
+        multiply(0, shifted_a, acc_a)
+        build(0, jnp.minimum(pair + 1, 1), shifted_a)
+        multiply(1, shifted_b, acc_a)
+        reduce(pair, acc_a)
+        return carry
 
     build(0, 0, shifted_a)
-    build(1, 0, shifted_b)
-    multiply(0, shifted_a, acc_a)
-    build(0, 1, shifted_a)
-    multiply(1, shifted_b, acc_a)
-    build(1, 1, shifted_b)
-    multiply(0, shifted_a, acc_b)
-    reduce(0, acc_a)
-    multiply(1, shifted_b, acc_b)
-    reduce(1, acc_b)
+    lax.fori_loop(0, 2, step, 0)
 
     values = score[...].reshape(ROT, ALL_C, 128) - quad[None]
     high = jnp.max(values, axis=0)
@@ -416,7 +425,6 @@
             pltpu.VMEM((2, 2 * SHIFTS, NB * KT), bf16),
             pltpu.VMEM((2, 2 * SHIFTS, NB * KT), bf16),
             pltpu.VMEM((2, HROWS, 2 * SHIFTS), f32),
-            pltpu.VMEM((2, HROWS, 2 * SHIFTS), f32),
             pltpu.VMEM((ROWS, 128), f32),
             pltpu.VMEM((128, CYCLES), f32),
             pltpu.VMEM((128, 128), f32),

time: 45.2 us -> 45.4 us (level)
  no operation moved by 1% of the time
where the time goes in v4:
time: 45.4 us; the launch traced here: 45.2 us
  Pallas kernels  43.3 us (95%)
  local copies, waits for them, and re-layouts  1.25 us (3%)
  between operations  0.64 us (1%)
    pallas_call x1, Pallas kernels, body(): pl.pallas_call(kernel, out_shape=(jax.ShapeDtypeStruct((16, LOCAL), f32),...  43.3 us

profile of v4, /device:TPU:24, one launch (start us, length us, event | category | flops | bytes accessed | tf_op | source)
XLA Modules:
  0.0 45.2 jit_solution(8863224812444305753)
XLA Ops:
  0.6 43.3 %expectation.1 = (f32[16,4]{1,0:T(8,128)S(1)}, f32[16,36]{1,0:T(8,128)S(1)}) custom-call(bf16[18,128,128]{2,1,0:T(8,128)(2,1)} %constant.4.clone.cos_hbm, bf16[18,128,128]{2,1,0:T(8,128)(2,1)} %constant.5.clone.sin_hbm, f32[16,144]{1,0:T(8,128)} %images_hbm.1, bf16[4,9216]{1,0:T(4,128)(2,1)} %references_hbm.1, f32[32,32]{1,0:T(8,128)} %ctf_hbm.1, ...), custom_call_target="tpu_custom_call" | custom-call | tf_op jit(solution)/shard_map/expectation/pallas_call | solution.py:389
  44.0 0.7 %copy.11 = f32[16,4]{0,1:T(4,128)} copy(f32[16,4]{1,0:T(8,128)S(1)} %get-tuple-element.2) | data formatting | bytes 512 | tf_op jit(solution)/shard_map/expectation/pallas_call | solution.py:389
  44.6 0.6 %copy.13 = f32[16,36]{1,0:T(8,128)} copy(f32[16,36]{1,0:T(8,128)S(1)} %get-tuple-element.7) | data formatting | bytes 4608

commit v5 on v4

--- a/solution.py
+++ b/solution.py
@@ -186,9 +186,6 @@
     left, right = (x + NX - 1) & (NX - 1), (x + 1) & (NX - 1)
     opposite = (x + 2) & (NX - 1)
     part_a, part_b = pl.ds(0, 40), pl.ds(40, HREF - 40)
-    slot = rall.at[x, core]
-    from_left = send(slot, slot, rsend.at[0], rrecv.at[0], right * NZ + z)
-    from_right = send(slot, slot, rsend.at[1], rrecv.at[1], left * NZ + z)
 
     for copy in x_copies:
         copy.wait_recv()
@@ -203,7 +200,11 @@
     gathered[z, 8, 0:1, :] = last[0:1] + moved[1:2]
     gathered[z, 8, 1:2, :] = last[2:3] + moved[3:4]
     z_copies = spread_z(gathered, zsend, zrecv, x, z)
-
+    slot = rall.at[x, core]
+    from_left = send(slot, slot, rsend.at[0], rrecv.at[0], right * NZ + z)
+    from_right = send(slot, slot, rsend.at[1], rrecv.at[1], left * NZ + z)
+
+    relay_z(gathered, zsend, zrecv, x, z, z_copies)
     from_left.wait_recv()
     slot = rall.at[left, core]
     part = rall.at[left, core, part_a]
@@ -214,7 +215,6 @@
     part = rall.at[right, core, part_b]
     onward_b = send(part, part, rsend.at[3], rrecv.at[3], left * NZ + z)
     over_right = send(slot, slot, rsend.at[5], rrecv.at[5], me, ptl=sibling)
-    relay_z(gathered, zsend, zrecv, x, z, z_copies)
     rho = iota((ROWS, 1), 0)
     kappa = ((rho >> 2) & 3) * (ROT * LOCAL) + (rho >> 4) * LOCAL + (rho & 3)
     place = (iota((ROWS, ROWS), 1) == kappa).astype(jnp.float32).astype(jnp.bfloat16)

time: 45.4 us -> 46.8 us (1.031); the launches traced: 45.2 us -> 46 us
  Pallas kernels: 43.3 us -> 44.1 us
    pallas_call x1, Pallas kernels: 43.3 us -> 44.1 us  [body(): pl.pallas_call(kernel, out_shape=(jax.ShapeDtypeStruct((16, LOCAL), f32),...]
where the time goes in v5:
time: 46.8 us; the launch traced here: 46 us
  Pallas kernels  44.1 us (94%)
  local copies, waits for them, and re-layouts  1.25 us (3%)
  between operations  0.64 us (1%)
    pallas_call x1, Pallas kernels, body(): pl.pallas_call(kernel, out_shape=(jax.ShapeDtypeStruct((16, LOCAL), f32),...  44.1 us

profile of v5, /device:TPU:24, one launch (start us, length us, event | category | flops | bytes accessed | tf_op | source)
XLA Modules:
  0.0 46.0 jit_solution(261305478932276113)
XLA Ops:
  0.6 44.1 %expectation.1 = (f32[16,4]{1,0:T(8,128)S(1)}, f32[16,36]{1,0:T(8,128)S(1)}) custom-call(bf16[18,128,128]{2,1,0:T(8,128)(2,1)} %constant.4.clone.cos_hbm, bf16[18,128,128]{2,1,0:T(8,128)(2,1)} %constant.5.clone.sin_hbm, f32[16,144]{1,0:T(8,128)} %images_hbm.1, bf16[4,9216]{1,0:T(4,128)(2,1)} %references_hbm.1, f32[32,32]{1,0:T(8,128)} %ctf_hbm.1, ...), custom_call_target="tpu_custom_call" | custom-call | tf_op jit(solution)/shard_map/expectation/pallas_call | solution.py:389
  44.8 0.7 %copy.11 = f32[16,4]{0,1:T(4,128)} copy(f32[16,4]{1,0:T(8,128)S(1)} %get-tuple-element.2) | data formatting | bytes 512 | tf_op jit(solution)/shard_map/expectation/pallas_call | solution.py:389
  45.4 0.6 %copy.13 = f32[16,36]{1,0:T(8,128)} copy(f32[16,36]{1,0:T(8,128)S(1)} %get-tuple-element.7) | data formatting | bytes 4608

commit v6 on v4

--- a/solution.py
+++ b/solution.py
@@ -18,14 +18,12 @@
 LOCAL = 4
 MINE = 4
 ALL_C = NX * LOCAL
-ROWS = ROT * ALL_C
 KT = 256
 NB = 9
 HALF = ROT // 2
 HREF = ROT * LOCAL // 2
 CHUNKS = HALF // NB
-HROWS = HALF * ALL_C
-WIDE = (2 * HALF - NB) * ALL_C
+BLOCK = 80
 NEAR = 4
 MESH = pl.DeviceIdType.MESH
 HIGH = lax.Precision.HIGHEST
@@ -96,7 +94,7 @@
     class_post, rot_post,
     cos, sin, images, references, ctf, noise, group, mic, count,
     rows_c, rows_n, rows_s, padded, split_a, split_b, xs, xr, main, tail, rall, gathered, cross,
-    turned, ends, wide, zt, mixed, shifted_a, shifted_b, acc_a, score, half, flip, tiles, post, outs,
+    ends, matrix, power, zt, mixed, shifted_a, shifted_b, acc_a, score, lines, half, flip, tiles, post, outs,
     local, xsend, xrecv, rsend, rrecv, zsend, zrecv, tsend, trecv, osend, orecv,
 ):
     me = lax.axis_index("cls")
@@ -118,6 +116,44 @@
     loads = [pltpu.make_async_copy(a, b, local.at[n]) for n, (a, b) in enumerate(pairs)]
     for load in loads:
         load.start()
+
+    loads[6].wait()
+    def divide(m, carry):
+        for n in range(8):
+            base = pl.multiple_of(8 * ANG * m + ANG * n // 128 * 128, 128)
+            block = references[:, pl.ds(base, 256)].astype(jnp.float32)
+            if n:
+                block = pltpu.roll(block, 256 - 16 * n, 1)
+            split_a[pl.ds(8 * m + n, LOCAL, stride=2 * CYCLES), :] = block[:, 0:128]
+            split_b[pl.ds(8 * m + n, LOCAL, stride=2 * CYCLES), :] = block[:, 128:256]
+        return carry
+
+    lax.fori_loop(0, 2 * CYCLES // 8, divide, 0)
+    rho = iota((KT, 1), 0)
+    repeat = (iota((KT, 2 * CYCLES), 1) == (rho >> 2)).astype(jnp.float32).astype(jnp.bfloat16)
+    angle = iota((1, 256), 1)
+    keep = ((rho & 3) == (angle & 3)) & (angle < ANG)
+    rho = iota((ROT * LOCAL, 1), 0)
+    block_of = jnp.where(rho < LOCAL, 0, ROT - (rho >> 2))
+    hit = (angle >> 2) == block_of
+    total = jnp.zeros((ROT * LOCAL, KT), jnp.float32)
+    for c in range(LOCAL):
+        cut = slice(2 * CYCLES * c, 2 * CYCLES * (c + 1))
+        one = jnp.concatenate([split_a[cut, :], split_b[cut, :]], axis=1).astype(jnp.bfloat16)
+        spread = jnp.dot(repeat, one, preferred_element_type=jnp.float32)
+        spread = jnp.where(keep, spread, 0.0).astype(jnp.bfloat16)
+        pick = (hit & ((rho & 3) == c)).astype(jnp.float32).astype(jnp.bfloat16)
+        total += lax.dot_general(pick, spread, NT, preferred_element_type=jnp.float32)
+    rall[x, 0] = total[0:HREF]
+    rall[x, 1] = total[HREF:]
+
+    pl.semaphore_wait(barrier, NX + 2 * NEAR)
+    left, right = (x + NX - 1) & (NX - 1), (x + 1) & (NX - 1)
+    opposite = (x + 2) & (NX - 1)
+    part_a, part_b = pl.ds(0, 40), pl.ds(40, HREF - 40)
+    slot = rall.at[x, core]
+    from_left = send(slot, slot, rsend.at[0], rrecv.at[0], right * NZ + z)
+    from_right = send(slot, slot, rsend.at[1], rrecv.at[1], left * NZ + z)
 
     for load in loads[:6]:
         load.wait()
@@ -135,6 +171,7 @@
     padded[...] = jnp.zeros_like(padded)
     tail[...] = jnp.zeros_like(tail)
     score[...] = jnp.zeros_like(score)
+    ends[:, :, 2 * HREF :, :] = jnp.zeros((2, 2, 8, 128), jnp.float32)
     padded[:, 0:ANG] = images[...] * column
     full = padded[...]
     row, lane = iota((16, 256), 0) & 3, iota((16, 256), 1) & 3
@@ -147,48 +184,31 @@
             line = jnp.sum(value[4 * t : 4 * t + 4], axis=0, keepdims=True)
             xs[t, d : d + 1, :] = line[:, 0:128]
             xs[t, 4 + d : 5 + d, :] = line[:, 128:256]
-
-    loads[6].wait()
-    def divide(m, carry):
-        for n in range(8):
-            base = pl.multiple_of(8 * ANG * m + ANG * n // 128 * 128, 128)
-            block = references[:, pl.ds(base, 256)].astype(jnp.float32)
-            if n:
-                block = pltpu.roll(block, 256 - 16 * n, 1)
-            split_a[pl.ds(8 * m + n, LOCAL, stride=2 * CYCLES), :] = block[:, 0:128]
-            split_b[pl.ds(8 * m + n, LOCAL, stride=2 * CYCLES), :] = block[:, 128:256]
-        return carry
-
-    lax.fori_loop(0, 2 * CYCLES // 8, divide, 0)
-    rho = iota((KT, 1), 0)
-    repeat = (iota((KT, 2 * CYCLES), 1) == (rho >> 2)).astype(jnp.float32).astype(jnp.bfloat16)
-    angle = iota((1, 256), 1)
-    keep = ((rho & 3) == (angle & 3)) & (angle < ANG)
-    rho = iota((ROT * LOCAL, 1), 0)
-    block_of = jnp.where(rho < LOCAL, 0, ROT - (rho >> 2))
-    hit = (angle >> 2) == block_of
-    total = jnp.zeros((ROT * LOCAL, KT), jnp.float32)
-    for c in range(LOCAL):
-        lines = slice(2 * CYCLES * c, 2 * CYCLES * (c + 1))
-        one = jnp.concatenate([split_a[lines, :], split_b[lines, :]], axis=1).astype(jnp.bfloat16)
-        spread = jnp.dot(repeat, one, preferred_element_type=jnp.float32)
-        spread = jnp.where(keep, spread, 0.0).astype(jnp.bfloat16)
-        pick = (hit & ((rho & 3) == c)).astype(jnp.float32).astype(jnp.bfloat16)
-        total += lax.dot_general(pick, spread, NT, preferred_element_type=jnp.float32)
-    rall[x, 0] = total[0:HREF]
-    rall[x, 1] = total[HREF:]
-
-    pl.semaphore_wait(barrier, NX + 2 * NEAR)
     x_copies = []
     for n, device in enumerate(along_x):
         x_copies.append(send(xs.at[(x + n + 1) & (NX - 1)], xr.at[x], xsend.at[n], xrecv.at[n], device))
     xr[x] = xs[x]
-    left, right = (x + NX - 1) & (NX - 1), (x + 1) & (NX - 1)
-    opposite = (x + 2) & (NX - 1)
-    part_a, part_b = pl.ds(0, 40), pl.ds(40, HREF - 40)
-    slot = rall.at[x, core]
-    from_left = send(slot, slot, rsend.at[0], rrecv.at[0], right * NZ + z)
-    from_right = send(slot, slot, rsend.at[1], rrecv.at[1], left * NZ + z)
+
+    def place(t):
+        low, high = rall[t, 0], rall[t, 1]
+        plus, minus = low + high, low - high
+        for lanes in range(2):
+            cut = slice(128 * lanes, 128 * lanes + 128)
+            ends[0, lanes, 0:HREF, :] = plus[:, cut]
+            ends[0, lanes, HREF : 2 * HREF, :] = plus[:, cut]
+            ends[1, lanes, 0:HREF, :] = -minus[:, cut]
+            ends[1, lanes, HREF : 2 * HREF, :] = minus[:, cut]
+        rows = pl.ds(pl.multiple_of(BLOCK * t, 16), BLOCK)
+        for sign in range(2):
+            for chunk in range(CHUNKS):
+                for q in range(NB):
+                    first = LOCAL * (HALF - NB * chunk - q)
+                    for lanes in range(2):
+                        at = KT * q + 128 * lanes
+                        value = ends[sign, lanes, first : first + BLOCK, :]
+                        matrix[sign, chunk, rows, at : at + 128] = value.astype(jnp.bfloat16)
+        square = jnp.sum((low * low + high * high).reshape(HREF // 8, 8, KT), axis=0)
+        power[pl.ds(pl.multiple_of(8 * t, 8), 8), :] = square + pltpu.roll(square, 4, 0)
 
     for copy in x_copies:
         copy.wait_recv()
@@ -215,41 +235,24 @@
     onward_b = send(part, part, rsend.at[3], rrecv.at[3], left * NZ + z)
     over_right = send(slot, slot, rsend.at[5], rrecv.at[5], me, ptl=sibling)
     relay_z(gathered, zsend, zrecv, x, z, z_copies)
-    rho = iota((ROWS, 1), 0)
-    kappa = ((rho >> 2) & 3) * (ROT * LOCAL) + (rho >> 4) * LOCAL + (rho & 3)
-    place = (iota((ROWS, ROWS), 1) == kappa).astype(jnp.float32).astype(jnp.bfloat16)
+    place(x)
     onward_a.wait_recv()
     onward_b.wait_recv()
     slot = rall.at[opposite, core]
     over_opposite = send(slot, slot, rsend.at[6], rrecv.at[6], me, ptl=sibling)
-    for copy in (over_left, over_right, over_opposite):
-        copy.wait_recv()
-
-    stacked = rall[...].reshape(ROWS, KT).astype(jnp.bfloat16)
-    turned[...] = jnp.dot(place, stacked, preferred_element_type=jnp.float32)
-
-    near_half, far_half = turned[0:HROWS, :], turned[HROWS:ROWS, :]
-    plus = (near_half + far_half).astype(jnp.bfloat16)
-    minus = (near_half - far_half).astype(jnp.bfloat16)
-    ends[0, 0:HROWS, :] = plus
-    ends[0, HROWS:ROWS, :] = plus
-    ends[1, 0:HROWS, :] = -minus
-    ends[1, HROWS:ROWS, :] = minus
-    for sign in range(2):
-        for q in range(NB):
-            first = ALL_C * (NB - q)
-            wide[sign, :, q * KT : (q + 1) * KT] = ends[sign, first : first + WIDE, :]
-
-    power = jnp.zeros((ALL_C, KT), jnp.float32)
-    for i in range(ROT):
-        line = turned[16 * i : 16 * i + 16, :]
-        power += line * line
+    over_left.wait_recv()
+    place(left)
+    over_right.wait_recv()
+    place(right)
+    over_opposite.wait_recv()
+    place(opposite)
+
     half[...] = jnp.zeros_like(half)
     half[0:MINE, :] = cross[pl.ds(x * MINE, MINE), :]
     lam = iota((1, KT), 1)
     spread = (iota((CYCLES, KT), 0) == ((lam >> 2) & 31)).astype(jnp.float32)
     half_wide = jnp.dot(half[...], spread, precision=HIGH, preferred_element_type=jnp.float32)
-    quad = lax.dot_general(power, half_wide, NT, precision=HIGH, preferred_element_type=jnp.float32)
+    quad = lax.dot_general(power[...], half_wide, NT, precision=HIGH, preferred_element_type=jnp.float32)
     loads[7].wait()
     loads[8].wait()
 
@@ -292,37 +295,33 @@
                 target[1, rows, right] = (s * rp - c * im).astype(jnp.bfloat16)
 
     def multiply(chunk, source, acc):
-        start = ALL_C * NB * (CHUNKS - 1 - chunk)
         for sign in range(2):
-            left = wide[sign, start : start + HROWS, :]
-            part = lax.dot_general(left, source[sign], NT, preferred_element_type=jnp.float32)
+            part = lax.dot_general(matrix[sign, chunk], source[sign], NT, preferred_element_type=jnp.float32)
             if chunk:
                 acc[sign] += part
             else:
                 acc[sign] = part
 
     def reduce(pair, acc):
-        size = 48
-        lane = iota((size, 128), 1)
-
-        def part(m, carry):
-            first = pl.multiple_of(m * size, 16)
-            tops = [jnp.zeros((size, 128), jnp.float32)] * 2
-            totals = [jnp.ones((size, 128), jnp.float32)] * 2
+        lane = iota((BLOCK, 128), 1)
+
+        def part(t, carry):
+            rows = pl.ds(pl.multiple_of(BLOCK * t, 16), BLOCK)
+            tops = [jnp.zeros((BLOCK, 128), jnp.float32)] * 2
+            totals = [jnp.ones((BLOCK, 128), jnp.float32)] * 2
             for h in range(2):
-                even = acc[0, pl.ds(first, size), 128 * h : 128 * h + 128]
-                odd = acc[1, pl.ds(first, size), 128 * h : 128 * h + 128]
+                even = acc[0, rows, 128 * h : 128 * h + 128]
+                odd = acc[1, rows, 128 * h : 128 * h + 128]
                 for half, value in enumerate((even + odd, even - odd)):
                     high = jnp.max(value, axis=1, keepdims=True)
                     low = jnp.sum(jnp.exp(value - high), axis=1, keepdims=True)
                     tops[half] = jnp.where(lane == 2 * pair + h, high, tops[half])
                     totals[half] = jnp.where(lane == 2 * pair + h, low, totals[half])
             for half in range(2):
-                rows = pl.ds(pl.multiple_of(half * HROWS + first, 16), size)
-                score[rows, :] += tops[half] + jnp.log(totals[half])
+                score[half, rows, :] += tops[half] + jnp.log(totals[half])
             return carry
 
-        lax.fori_loop(0, HROWS // size, part, 0, unroll=2)
+        lax.fori_loop(0, NX, part, 0)
 
     def step(pair, carry):
         build(1, pair, shifted_b)
@@ -335,14 +334,28 @@
     build(0, 0, shifted_a)
     lax.fori_loop(0, 2, step, 0)
 
-    values = score[...].reshape(ROT, ALL_C, 128) - quad[None]
-    high = jnp.max(values, axis=0)
-    by_class = high + jnp.log(jnp.sum(jnp.exp(values - high[None]), axis=0))
-    high = jnp.max(values, axis=1)
-    by_rot = high + jnp.log(jnp.sum(jnp.exp(values - high[:, None]), axis=1))
+    tiles_of = (HREF // 8, 8, 128)
     flip[...] = jnp.zeros_like(flip)
-    flip[0:ROT, :] = by_rot
-    flip[64 : 64 + ALL_C, :] = by_class
+    values = []
+    for t in range(NX):
+        shift = quad[8 * t : 8 * t + 8]
+        pair = [score[half, BLOCK * t : BLOCK * t + HREF, :].reshape(tiles_of) - shift for half in range(2)]
+        values.append(pair)
+        high = jnp.maximum(jnp.max(pair[0], axis=0), jnp.max(pair[1], axis=0))
+        high = jnp.maximum(high, pltpu.roll(high, 4, 0))
+        low = jnp.sum(jnp.exp(pair[0] - high), axis=0) + jnp.sum(jnp.exp(pair[1] - high), axis=0)
+        low = low + pltpu.roll(low, 4, 0)
+        by_class = high + jnp.log(low)
+        flip[64 + LOCAL * t : 64 + LOCAL * (t + 1), :] = by_class[0:LOCAL]
+    for half in range(2):
+        four = [values[t][half] for t in range(NX)]
+        high = jnp.maximum(jnp.maximum(four[0], four[1]), jnp.maximum(four[2], four[3]))
+        low = jnp.exp(four[0] - high) + jnp.exp(four[1] - high) + jnp.exp(four[2] - high) + jnp.exp(four[3] - high)
+        lines[half * HREF : (half + 1) * HREF, :] = (high + jnp.log(low)).reshape(HREF, 128)
+    four = [lines[pl.ds(c, ROT, stride=LOCAL), :] for c in range(LOCAL)]
+    high = jnp.maximum(jnp.maximum(four[0], four[1]), jnp.maximum(four[2], four[3]))
+    low = jnp.exp(four[0] - high) + jnp.exp(four[1] - high) + jnp.exp(four[2] - high) + jnp.exp(four[3] - high)
+    flip[0:ROT, :] = high + jnp.log(low)
     tile = flip[...].T[0:MINE, :]
 
     tiles[z] = tile
@@ -417,15 +430,16 @@
             pltpu.VMEM((NX, 2, HREF, KT), f32),
             pltpu.VMEM((NZ, 9, 2, 128), f32),
             pltpu.VMEM((16, CYCLES), f32),
-            pltpu.VMEM((ROWS, KT), f32),
-            pltpu.VMEM((2, ROWS, KT), bf16),
-            pltpu.VMEM((2, WIDE, NB * KT), bf16),
+            pltpu.VMEM((2, 2, 2 * HREF + 8, 128), f32),
+            pltpu.VMEM((2, CHUNKS, NX * BLOCK, NB * KT), bf16),
+            pltpu.VMEM((NX * 8, KT), f32),
             pltpu.VMEM((2, ANG, 128), f32),
             pltpu.VMEM((2, 2, ANG // 2, 128), f32),
             pltpu.VMEM((2, 2 * SHIFTS, NB * KT), bf16),
             pltpu.VMEM((2, 2 * SHIFTS, NB * KT), bf16),
-            pltpu.VMEM((2, HROWS, 2 * SHIFTS), f32),
-            pltpu.VMEM((ROWS, 128), f32),
+            pltpu.VMEM((2, NX * BLOCK, 2 * SHIFTS), f32),
+            pltpu.VMEM((2, NX * BLOCK, 128), f32),
+            pltpu.VMEM((2 * HREF, 128), f32),
             pltpu.VMEM((128, CYCLES), f32),
             pltpu.VMEM((128, 128), f32),
             pltpu.VMEM((NZ, MINE, 128), f32),

time: 45.4 us -> 46.4 us (1.022)
  Pallas kernels: 43.3 us -> 44.3 us
    pallas_call x1, Pallas kernels: 43.3 us -> 44.3 us  [body(): pl.pallas_call(kernel, out_shape=(jax.ShapeDtypeStruct((16, LOCAL), f32),...]
where the time goes in v6:
time: 46.4 us; the launch traced here: 46.2 us
  Pallas kernels  44.3 us (95%)
  local copies, waits for them, and re-layouts  1.25 us (3%)
  between operations  0.64 us (1%)
    pallas_call x1, Pallas kernels, body(): pl.pallas_call(kernel, out_shape=(jax.ShapeDtypeStruct((16, LOCAL), f32),...  44.3 us

profile of v6, /device:TPU:24, one launch (start us, length us, event | category | flops | bytes accessed | tf_op | source)
XLA Modules:
  0.0 46.2 jit_solution(12526622410505829303)
XLA Ops:
  0.6 44.3 %expectation.1 = (f32[16,4]{1,0:T(8,128)S(1)}, f32[16,36]{1,0:T(8,128)S(1)}) custom-call(bf16[18,128,128]{2,1,0:T(8,128)(2,1)} %constant.4.clone.cos_hbm, bf16[18,128,128]{2,1,0:T(8,128)(2,1)} %constant.5.clone.sin_hbm, f32[16,144]{1,0:T(8,128)} %images_hbm.1, bf16[4,9216]{1,0:T(4,128)(2,1)} %references_hbm.1, f32[32,32]{1,0:T(8,128)} %ctf_hbm.1, ...), custom_call_target="tpu_custom_call" | custom-call | tf_op jit(solution)/shard_map/expectation/pallas_call | solution.py:402
  45.0 0.7 %copy.11 = f32[16,4]{0,1:T(4,128)} copy(f32[16,4]{1,0:T(8,128)S(1)} %get-tuple-element.2) | data formatting | bytes 512 | tf_op jit(solution)/shard_map/expectation/pallas_call | solution.py:402
  45.6 0.6 %copy.13 = f32[16,36]{1,0:T(8,128)} copy(f32[16,36]{1,0:T(8,128)S(1)} %get-tuple-element.7) | data formatting | bytes 4608

commit v7 on v6

--- a/solution.py
+++ b/solution.py
@@ -116,44 +116,6 @@
     loads = [pltpu.make_async_copy(a, b, local.at[n]) for n, (a, b) in enumerate(pairs)]
     for load in loads:
         load.start()
-
-    loads[6].wait()
-    def divide(m, carry):
-        for n in range(8):
-            base = pl.multiple_of(8 * ANG * m + ANG * n // 128 * 128, 128)
-            block = references[:, pl.ds(base, 256)].astype(jnp.float32)
-            if n:
-                block = pltpu.roll(block, 256 - 16 * n, 1)
-            split_a[pl.ds(8 * m + n, LOCAL, stride=2 * CYCLES), :] = block[:, 0:128]
-            split_b[pl.ds(8 * m + n, LOCAL, stride=2 * CYCLES), :] = block[:, 128:256]
-        return carry
-
-    lax.fori_loop(0, 2 * CYCLES // 8, divide, 0)
-    rho = iota((KT, 1), 0)
-    repeat = (iota((KT, 2 * CYCLES), 1) == (rho >> 2)).astype(jnp.float32).astype(jnp.bfloat16)
-    angle = iota((1, 256), 1)
-    keep = ((rho & 3) == (angle & 3)) & (angle < ANG)
-    rho = iota((ROT * LOCAL, 1), 0)
-    block_of = jnp.where(rho < LOCAL, 0, ROT - (rho >> 2))
-    hit = (angle >> 2) == block_of
-    total = jnp.zeros((ROT * LOCAL, KT), jnp.float32)
-    for c in range(LOCAL):
-        cut = slice(2 * CYCLES * c, 2 * CYCLES * (c + 1))
-        one = jnp.concatenate([split_a[cut, :], split_b[cut, :]], axis=1).astype(jnp.bfloat16)
-        spread = jnp.dot(repeat, one, preferred_element_type=jnp.float32)
-        spread = jnp.where(keep, spread, 0.0).astype(jnp.bfloat16)
-        pick = (hit & ((rho & 3) == c)).astype(jnp.float32).astype(jnp.bfloat16)
-        total += lax.dot_general(pick, spread, NT, preferred_element_type=jnp.float32)
-    rall[x, 0] = total[0:HREF]
-    rall[x, 1] = total[HREF:]
-
-    pl.semaphore_wait(barrier, NX + 2 * NEAR)
-    left, right = (x + NX - 1) & (NX - 1), (x + 1) & (NX - 1)
-    opposite = (x + 2) & (NX - 1)
-    part_a, part_b = pl.ds(0, 40), pl.ds(40, HREF - 40)
-    slot = rall.at[x, core]
-    from_left = send(slot, slot, rsend.at[0], rrecv.at[0], right * NZ + z)
-    from_right = send(slot, slot, rsend.at[1], rrecv.at[1], left * NZ + z)
 
     for load in loads[:6]:
         load.wait()
@@ -184,10 +146,49 @@
             line = jnp.sum(value[4 * t : 4 * t + 4], axis=0, keepdims=True)
             xs[t, d : d + 1, :] = line[:, 0:128]
             xs[t, 4 + d : 5 + d, :] = line[:, 128:256]
+
+    pl.semaphore_wait(barrier, NX + 2 * NEAR)
     x_copies = []
     for n, device in enumerate(along_x):
         x_copies.append(send(xs.at[(x + n + 1) & (NX - 1)], xr.at[x], xsend.at[n], xrecv.at[n], device))
     xr[x] = xs[x]
+
+    loads[6].wait()
+    def divide(m, carry):
+        for n in range(8):
+            base = pl.multiple_of(8 * ANG * m + ANG * n // 128 * 128, 128)
+            block = references[:, pl.ds(base, 256)].astype(jnp.float32)
+            if n:
+                block = pltpu.roll(block, 256 - 16 * n, 1)
+            split_a[pl.ds(8 * m + n, LOCAL, stride=2 * CYCLES), :] = block[:, 0:128]
+            split_b[pl.ds(8 * m + n, LOCAL, stride=2 * CYCLES), :] = block[:, 128:256]
+        return carry
+
+    lax.fori_loop(0, 2 * CYCLES // 8, divide, 0)
+    rho = iota((KT, 1), 0)
+    repeat = (iota((KT, 2 * CYCLES), 1) == (rho >> 2)).astype(jnp.float32).astype(jnp.bfloat16)
+    angle = iota((1, 256), 1)
+    keep = ((rho & 3) == (angle & 3)) & (angle < ANG)
+    rho = iota((ROT * LOCAL, 1), 0)
+    block_of = jnp.where(rho < LOCAL, 0, ROT - (rho >> 2))
+    hit = (angle >> 2) == block_of
+    total = jnp.zeros((ROT * LOCAL, KT), jnp.float32)
+    for c in range(LOCAL):
+        cut = slice(2 * CYCLES * c, 2 * CYCLES * (c + 1))
+        one = jnp.concatenate([split_a[cut, :], split_b[cut, :]], axis=1).astype(jnp.bfloat16)
+        spread = jnp.dot(repeat, one, preferred_element_type=jnp.float32)
+        spread = jnp.where(keep, spread, 0.0).astype(jnp.bfloat16)
+        pick = (hit & ((rho & 3) == c)).astype(jnp.float32).astype(jnp.bfloat16)
+        total += lax.dot_general(pick, spread, NT, preferred_element_type=jnp.float32)
+    rall[x, 0] = total[0:HREF]
+    rall[x, 1] = total[HREF:]
+
+    left, right = (x + NX - 1) & (NX - 1), (x + 1) & (NX - 1)
+    opposite = (x + 2) & (NX - 1)
+    part_a, part_b = pl.ds(0, 40), pl.ds(40, HREF - 40)
+    slot = rall.at[x, core]
+    from_left = send(slot, slot, rsend.at[0], rrecv.at[0], right * NZ + z)
+    from_right = send(slot, slot, rsend.at[1], rrecv.at[1], left * NZ + z)
 
     def place(t):
         low, high = rall[t, 0], rall[t, 1]

time: 46.4 us -> 45.6 us (0.983)
  Pallas kernels: 44.3 us -> 43.5 us
    pallas_call x1, Pallas kernels: 44.3 us -> 43.5 us  [body(): pl.pallas_call(kernel, out_shape=(jax.ShapeDtypeStruct((16, LOCAL), f32),...]
where the time goes in v7:
time: 45.6 us; the launch traced here: 45.4 us
  Pallas kernels  43.5 us (95%)
  local copies, waits for them, and re-layouts  1.25 us (3%)
  between operations  0.64 us (1%)
    pallas_call x1, Pallas kernels, body(): pl.pallas_call(kernel, out_shape=(jax.ShapeDtypeStruct((16, LOCAL), f32),...  43.5 us

profile of v7, /device:TPU:24, one launch (start us, length us, event | category | flops | bytes accessed | tf_op | source)
XLA Modules:
  0.0 45.4 jit_solution(9972409039927078277)
XLA Ops:
  0.6 43.5 %expectation.1 = (f32[16,4]{1,0:T(8,128)S(1)}, f32[16,36]{1,0:T(8,128)S(1)}) custom-call(bf16[18,128,128]{2,1,0:T(8,128)(2,1)} %constant.4.clone.cos_hbm, bf16[18,128,128]{2,1,0:T(8,128)(2,1)} %constant.5.clone.sin_hbm, f32[16,144]{1,0:T(8,128)} %images_hbm.1, bf16[4,9216]{1,0:T(4,128)(2,1)} %references_hbm.1, f32[32,32]{1,0:T(8,128)} %ctf_hbm.1, ...), custom_call_target="tpu_custom_call" | custom-call | tf_op jit(solution)/shard_map/expectation/pallas_call | solution.py:403
  44.2 0.7 %copy.11 = f32[16,4]{0,1:T(4,128)} copy(f32[16,4]{1,0:T(8,128)S(1)} %get-tuple-element.2) | data formatting | bytes 512 | tf_op jit(solution)/shard_map/expectation/pallas_call | solution.py:403
  44.8 0.6 %copy.13 = f32[16,36]{1,0:T(8,128)} copy(f32[16,36]{1,0:T(8,128)S(1)} %get-tuple-element.7) | data formatting | bytes 4608

commit v8 on v7

--- a/solution.py
+++ b/solution.py
@@ -19,10 +19,8 @@
 MINE = 4
 ALL_C = NX * LOCAL
 KT = 256
-NB = 9
 HALF = ROT // 2
 HREF = ROT * LOCAL // 2
-CHUNKS = HALF // NB
 BLOCK = 80
 NEAR = 4
 MESH = pl.DeviceIdType.MESH
@@ -40,7 +38,7 @@
     phase = 2.0 * math.pi * radius[:, None, None] * along[None]
 
     def order(table):
-        table = table.reshape(2, NZ, ROT, STEP, SHIFTS).transpose(2, 4, 0, 1, 3)
+        table = table.reshape(2, NZ, ROT, STEP, SHIFTS).transpose(2, 4, 1, 0, 3)
         return table.reshape(ROT, SHIFTS, 128)[:HALF].astype(jnp.bfloat16)
 
     return order(np.cos(phase)), order(np.sin(phase))
@@ -83,9 +81,9 @@
             copies[step] = send(slot, slot, sends.at[step % NZ], recvs.at[step % NZ], device)
 
 
-def arrive_z(copies):
+def arrive_z(copies, nearer):
     for step, copy in copies.items():
-        if abs(step) != NEAR:
+        if abs(step) != NEAR and (abs(step) < NEAR) == nearer:
             copy.wait_recv()
 
 
@@ -93,8 +91,8 @@
     cos_hbm, sin_hbm, images_hbm, references_hbm, ctf_hbm, noise_hbm, group_hbm, mic_hbm, count_hbm,
     class_post, rot_post,
     cos, sin, images, references, ctf, noise, group, mic, count,
-    rows_c, rows_n, rows_s, padded, split_a, split_b, xs, xr, main, tail, rall, gathered, cross,
-    ends, matrix, power, zt, mixed, shifted_a, shifted_b, acc_a, score, lines, half, flip, tiles, post, outs,
+    rows_c, rows_n, rows_s, padded, split_a, split_b, xs, xr, main, tail, ahead, rall, gathered, cross,
+    ends, matrix, power, zt, mixed, shifted_a, shifted_b, acc_a, acc_b, table_c, table_s, score, lines, half, flip, tiles, post, outs,
     local, xsend, xrecv, rsend, rrecv, zsend, zrecv, tsend, trecv, osend, orecv,
 ):
     me = lax.axis_index("cls")
@@ -166,7 +164,9 @@
 
     lax.fori_loop(0, 2 * CYCLES // 8, divide, 0)
     rho = iota((KT, 1), 0)
-    repeat = (iota((KT, 2 * CYCLES), 1) == (rho >> 2)).astype(jnp.float32).astype(jnp.bfloat16)
+    source = (z - 4 + ((rho >> 7) << 3) + ((rho >> 3) & 7)) & (NZ - 1)
+    kappa = (((rho >> 6) & 1) << 5) + (((rho >> 2) & 1) << 4) + source
+    repeat = (iota((KT, 2 * CYCLES), 1) == kappa).astype(jnp.float32).astype(jnp.bfloat16)
     angle = iota((1, 256), 1)
     keep = ((rho & 3) == (angle & 3)) & (angle < ANG)
     rho = iota((ROT * LOCAL, 1), 0)
@@ -201,29 +201,44 @@
             ends[1, lanes, HREF : 2 * HREF, :] = minus[:, cut]
         rows = pl.ds(pl.multiple_of(BLOCK * t, 16), BLOCK)
         for sign in range(2):
-            for chunk in range(CHUNKS):
-                for q in range(NB):
-                    first = LOCAL * (HALF - NB * chunk - q)
-                    for lanes in range(2):
-                        at = KT * q + 128 * lanes
-                        value = ends[sign, lanes, first : first + BLOCK, :]
-                        matrix[sign, chunk, rows, at : at + 128] = value.astype(jnp.bfloat16)
+            for b in range(HALF):
+                first = LOCAL * (HALF - b)
+                for lanes in range(2):
+                    value = ends[sign, lanes, first : first + BLOCK, :]
+                    matrix[sign, lanes, rows, 128 * b : 128 * b + 128] = value.astype(jnp.bfloat16)
         square = jnp.sum((low * low + high * high).reshape(HREF // 8, 8, KT), axis=0)
         power[pl.ds(pl.multiple_of(8 * t, 8), 8), :] = square + pltpu.roll(square, 4, 0)
 
     for copy in x_copies:
         copy.wait_recv()
-    last = jnp.zeros((STEP, 128), jnp.float32)
-    for t in range(NX):
-        block = xr[t]
-        gathered[z, 2 * t] = block[0:2]
-        gathered[z, 2 * t + 1] = block[2:4]
-        rest = block[4:8]
-        last = last + (pltpu.roll(rest, 16 * t, 1) if t else rest)
-    moved = pltpu.roll(last, 64, 1)
-    gathered[z, 8, 0:1, :] = last[0:1] + moved[1:2]
-    gathered[z, 8, 1:2, :] = last[2:3] + moved[3:4]
+    for part in range(2):
+        last = jnp.zeros((1, 128), jnp.float32)
+        for low in range(2):
+            t = 2 * part + low
+            block = xr[t]
+            gathered[z, 2 * t] = block[0:2]
+            gathered[z, 2 * t + 1] = block[2:4]
+            for d in range(STEP):
+                at = 16 * (STEP * low + d)
+                rest = block[4 + d : 5 + d]
+                last = last + (pltpu.roll(rest, at, 1) if at else rest)
+        gathered[z, 8, part : part + 1, :] = last
     z_copies = spread_z(gathered, zsend, zrecv, x, z)
+
+    loads[7].wait()
+    loads[8].wait()
+    first_lanes = iota((128, 128), 1) < 64
+    turn = ((20 - z) * 8) & 127
+
+    def arrange(b, carry):
+        for table, rolled_table, sign in ((cos, table_c, -1.0), (sin, table_s, 1.0)):
+            value = pltpu.roll(table[b].astype(jnp.float32), turn, 1)
+            moved = pltpu.roll(value, 64, 1)
+            rolled_table[0, b] = jnp.where(first_lanes, value, sign * moved)
+            rolled_table[1, b] = jnp.where(first_lanes, moved, sign * value)
+        return carry
+
+    lax.fori_loop(0, HALF, arrange, 0)
 
     from_left.wait_recv()
     slot = rall.at[left, core]
@@ -251,54 +266,48 @@
     half[...] = jnp.zeros_like(half)
     half[0:MINE, :] = cross[pl.ds(x * MINE, MINE), :]
     lam = iota((1, KT), 1)
-    spread = (iota((CYCLES, KT), 0) == ((lam >> 2) & 31)).astype(jnp.float32)
+    cycle = (((lam >> 2) & 1) << 4) + ((z - 4 + ((lam >> 7) << 3) + ((lam >> 3) & 7)) & (NZ - 1))
+    spread = (iota((CYCLES, KT), 0) == cycle).astype(jnp.float32)
     half_wide = jnp.dot(half[...], spread, precision=HIGH, preferred_element_type=jnp.float32)
     quad = lax.dot_general(power[...], half_wide, NT, precision=HIGH, preferred_element_type=jnp.float32)
-    loads[7].wait()
-    loads[8].wait()
-
-    arrive_z(z_copies)
-    for origin in range(NZ):
-        for t in range(NX):
-            row = 64 * (t % 2) + 4 * origin
-            main[t // 2, row : row + 2, :] = gathered[origin, 2 * t]
-            main[t // 2, row + 2 : row + 4, :] = gathered[origin, 2 * t + 1]
-        last = gathered[origin, 8]
-        moved = pltpu.roll(last, 64, 1)
-        row = 4 * origin
-        tail[row : row + 1, :] = last[0:1]
-        tail[row + 1 : row + 2, :] = moved[0:1]
-        tail[row + 2 : row + 3, :] = last[1:2]
-        tail[row + 3 : row + 4, :] = moved[1:2]
-    rest = tail[...].T
-    lane = iota((16, 128), 1)
-    for part in range(2):
-        zt[part, 0:128] = main[part].T
-        low, high = rest[32 * part : 32 * part + 16], rest[32 * part + 16 : 32 * part + 32]
-        zt[part, 128:ANG] = jnp.where(lane < 64, low, pltpu.roll(high, 64, 1))
-    for part in range(2):
-        one, two = zt[part, 0 : ANG // 2, :], zt[part, ANG // 2 : ANG, :]
-        mixed[part, 0] = 0.5 * (one + two)
-        mixed[part, 1] = 0.5 * (one - two)
-
-    def build(chunk, pair, target):
-        for q in range(NB):
-            b = chunk * NB + q
-            c, s = cos[b].astype(jnp.float32), sin[b].astype(jnp.float32)
-            left, right = slice(q * KT, q * KT + 128), slice(q * KT + 128, q * KT + 256)
+    def unpack(far):
+        for zr in range(8):
+            origin = (z - 4 + 8 * far + zr) & (NZ - 1)
+            for t in range(NX):
+                row = 64 * (t // 2) + 8 * zr + 4 * (t % 2)
+                main[row : row + 2, :] = gathered[origin, 2 * t]
+                main[row + 2 : row + 4, :] = gathered[origin, 2 * t + 1]
+            last = gathered[origin, 8]
+            ahead[zr : zr + 1, :] = last[0:1]
+            ahead[8 + zr : 9 + zr, :] = last[1:2]
+        last = ahead[...]
+        for n in range(8):
+            moved = pltpu.roll(last, 128 - 16 * n, 1) if n else last
+            tail[pl.ds(n, 8, stride=8), :] = moved[0:8]
+            tail[pl.ds(64 + n, 8, stride=8), :] = moved[8:16]
+        zt[0:128] = main[...].T
+        zt[128:ANG] = tail[...].T[0:16]
+        one, two = zt[0 : ANG // 2, :], zt[ANG // 2 : ANG, :]
+        plus, minus = 0.5 * (one + two), 0.5 * (one - two)
+        mixed[0] = plus
+        mixed[1] = minus
+        mixed[2] = pltpu.roll(plus, 64, 1)
+        mixed[3] = pltpu.roll(minus, 64, 1)
+
+    def build(far, pair, target):
+        for b in range(HALF):
+            c, s = table_c[far, b], table_s[far, b]
+            lanes = slice(128 * b, 128 * b + 128)
             for h in range(2):
-                line = pl.ds(4 * b + 2 * pair + h, 1)
-                rp, rm, ip, im = mixed[0, 0, line], mixed[0, 1, line], mixed[1, 0, line], mixed[1, 1, line]
+                line = slice(4 * b + 2 * pair + h, 4 * b + 2 * pair + h + 1)
                 rows = slice(128 * h, 128 * h + 128)
-                target[0, rows, left] = (c * rp + s * im).astype(jnp.bfloat16)
-                target[0, rows, right] = (s * rm - c * ip).astype(jnp.bfloat16)
-                target[1, rows, left] = (c * rm + s * ip).astype(jnp.bfloat16)
-                target[1, rows, right] = (s * rp - c * im).astype(jnp.bfloat16)
-
-    def multiply(chunk, source, acc):
+                target[0, rows, lanes] = (c * mixed[0, line] + s * mixed[3, line]).astype(jnp.bfloat16)
+                target[1, rows, lanes] = (c * mixed[1, line] + s * mixed[2, line]).astype(jnp.bfloat16)
+
+    def multiply(far, source, acc):
         for sign in range(2):
-            part = lax.dot_general(matrix[sign, chunk], source[sign], NT, preferred_element_type=jnp.float32)
-            if chunk:
+            part = lax.dot_general(matrix[sign, far], source[sign], NT, preferred_element_type=jnp.float32)
+            if far:
                 acc[sign] += part
             else:
                 acc[sign] = part
@@ -324,16 +333,15 @@
 
         lax.fori_loop(0, NX, part, 0)
 
-    def step(pair, carry):
-        build(1, pair, shifted_b)
-        multiply(0, shifted_a, acc_a)
-        build(0, jnp.minimum(pair + 1, 1), shifted_a)
-        multiply(1, shifted_b, acc_a)
-        reduce(pair, acc_a)
-        return carry
-
-    build(0, 0, shifted_a)
-    lax.fori_loop(0, 2, step, 0)
+    for far in range(2):
+        arrive_z(z_copies, far == 0)
+        unpack(far)
+        build(far, 0, shifted_a)
+        build(far, 1, shifted_b)
+        multiply(far, shifted_a, acc_a)
+        multiply(far, shifted_b, acc_b)
+    reduce(0, acc_a)
+    reduce(1, acc_b)
 
     tiles_of = (HREF // 8, 8, 128)
     flip[...] = jnp.zeros_like(flip)
@@ -426,19 +434,23 @@
             pltpu.VMEM((2 * CYCLES * LOCAL, 128), f32),
             pltpu.VMEM((NX, 8, 128), f32),
             pltpu.VMEM((NX, 8, 128), f32),
-            pltpu.VMEM((2, 128, 128), f32),
             pltpu.VMEM((128, 128), f32),
+            pltpu.VMEM((128, 128), f32),
+            pltpu.VMEM((16, 128), f32),
             pltpu.VMEM((NX, 2, HREF, KT), f32),
             pltpu.VMEM((NZ, 9, 2, 128), f32),
             pltpu.VMEM((16, CYCLES), f32),
             pltpu.VMEM((2, 2, 2 * HREF + 8, 128), f32),
-            pltpu.VMEM((2, CHUNKS, NX * BLOCK, NB * KT), bf16),
+            pltpu.VMEM((2, 2, NX * BLOCK, HALF * 128), bf16),
             pltpu.VMEM((NX * 8, KT), f32),
-            pltpu.VMEM((2, ANG, 128), f32),
-            pltpu.VMEM((2, 2, ANG // 2, 128), f32),
-            pltpu.VMEM((2, 2 * SHIFTS, NB * KT), bf16),
-            pltpu.VMEM((2, 2 * SHIFTS, NB * KT), bf16),
+            pltpu.VMEM((ANG, 128), f32),
+            pltpu.VMEM((4, ANG // 2, 128), f32),
+            pltpu.VMEM((2, 2 * SHIFTS, HALF * 128), bf16),
+            pltpu.VMEM((2, 2 * SHIFTS, HALF * 128), bf16),
             pltpu.VMEM((2, NX * BLOCK, 2 * SHIFTS), f32),
+            pltpu.VMEM((2, NX * BLOCK, 2 * SHIFTS), f32),
+            pltpu.VMEM((2, HALF, SHIFTS, 128), f32),
+            pltpu.VMEM((2, HALF, SHIFTS, 128), f32),
             pltpu.VMEM((2, NX * BLOCK, 128), f32),
             pltpu.VMEM((2 * HREF, 128), f32),
             pltpu.VMEM((128, CYCLES), f32),

time: 45.6 us -> 44.3 us (0.971); the launches traced: 45.4 us -> 43.5 us
  Pallas kernels: 43.5 us -> 41.6 us
    pallas_call x1, Pallas kernels: 43.5 us -> 41.6 us  [body(): pl.pallas_call(kernel, out_shape=(jax.ShapeDtypeStruct((16, LOCAL), f32),...]
where the time goes in v8:
time: 44.3 us; the launch traced here: 43.5 us
  Pallas kernels  41.6 us (94%)
  local copies, waits for them, and re-layouts  1.25 us (3%)
  between operations  0.64 us (1%)
    pallas_call x1, Pallas kernels, body(): pl.pallas_call(kernel, out_shape=(jax.ShapeDtypeStruct((16, LOCAL), f32),...  41.6 us

profile of v8, /device:TPU:24, one launch (start us, length us, event | category | flops | bytes accessed | tf_op | source)
XLA Modules:
  0.0 43.5 jit_solution(15026340898709825725)
XLA Ops:
  0.6 41.6 %expectation.1 = (f32[16,4]{1,0:T(8,128)S(1)}, f32[16,36]{1,0:T(8,128)S(1)}) custom-call(bf16[18,128,128]{2,1,0:T(8,128)(2,1)} %constant.4.clone.cos_hbm, bf16[18,128,128]{2,1,0:T(8,128)(2,1)} %constant.5.clone.sin_hbm, f32[16,144]{1,0:T(8,128)} %images_hbm.1, bf16[4,9216]{1,0:T(4,128)(2,1)} %references_hbm.1, f32[32,32]{1,0:T(8,128)} %ctf_hbm.1, ...), custom_call_target="tpu_custom_call" | custom-call | tf_op jit(solution)/shard_map/expectation/pallas_call | solution.py:411
  42.3 0.7 %copy.11 = f32[16,4]{0,1:T(4,128)} copy(f32[16,4]{1,0:T(8,128)S(1)} %get-tuple-element.2) | data formatting | bytes 512 | tf_op jit(solution)/shard_map/expectation/pallas_call | solution.py:411
  42.9 0.6 %copy.13 = f32[16,36]{1,0:T(8,128)} copy(f32[16,36]{1,0:T(8,128)S(1)} %get-tuple-element.7) | data formatting | bytes 4608

commit v9 on v8

--- a/solution.py
+++ b/solution.py
@@ -250,12 +250,12 @@
     part = rall.at[right, core, part_b]
     onward_b = send(part, part, rsend.at[3], rrecv.at[3], left * NZ + z)
     over_right = send(slot, slot, rsend.at[5], rrecv.at[5], me, ptl=sibling)
-    relay_z(gathered, zsend, zrecv, x, z, z_copies)
     place(x)
     onward_a.wait_recv()
     onward_b.wait_recv()
     slot = rall.at[opposite, core]
     over_opposite = send(slot, slot, rsend.at[6], rrecv.at[6], me, ptl=sibling)
+    relay_z(gathered, zsend, zrecv, x, z, z_copies)
     over_left.wait_recv()
     place(left)
     over_right.wait_recv()
@@ -263,13 +263,15 @@
     over_opposite.wait_recv()
     place(opposite)
 
-    half[...] = jnp.zeros_like(half)
-    half[0:MINE, :] = cross[pl.ds(x * MINE, MINE), :]
-    lam = iota((1, KT), 1)
-    cycle = (((lam >> 2) & 1) << 4) + ((z - 4 + ((lam >> 7) << 3) + ((lam >> 3) & 7)) & (NZ - 1))
-    spread = (iota((CYCLES, KT), 0) == cycle).astype(jnp.float32)
-    half_wide = jnp.dot(half[...], spread, precision=HIGH, preferred_element_type=jnp.float32)
-    quad = lax.dot_general(power[...], half_wide, NT, precision=HIGH, preferred_element_type=jnp.float32)
+    def quadratic():
+        half[...] = jnp.zeros_like(half)
+        half[0:MINE, :] = cross[pl.ds(x * MINE, MINE), :]
+        lam = iota((1, KT), 1)
+        cycle = (((lam >> 2) & 1) << 4) + ((z - 4 + ((lam >> 7) << 3) + ((lam >> 3) & 7)) & (NZ - 1))
+        spread = (iota((CYCLES, KT), 0) == cycle).astype(jnp.float32)
+        half_wide = jnp.dot(half[...], spread, precision=HIGH, preferred_element_type=jnp.float32)
+        return lax.dot_general(power[...], half_wide, NT, precision=HIGH, preferred_element_type=jnp.float32)
+
     def unpack(far):
         for zr in range(8):
             origin = (z - 4 + 8 * far + zr) & (NZ - 1)
@@ -340,6 +342,8 @@
         build(far, 1, shifted_b)
         multiply(far, shifted_a, acc_a)
         multiply(far, shifted_b, acc_b)
+        if far == 0:
+            quad = quadratic()
     reduce(0, acc_a)
     reduce(1, acc_b)
 

time: 44.3 us -> 45.6 us (1.029); the launches traced: 43.5 us -> 45.4 us
  Pallas kernels: 41.6 us -> 43.5 us
    pallas_call x1, Pallas kernels: 41.6 us -> 43.5 us  [body(): pl.pallas_call(kernel, out_shape=(jax.ShapeDtypeStruct((16, LOCAL), f32),...]
where the time goes in v9:
time: 45.6 us; the launch traced here: 45.4 us
  Pallas kernels  43.5 us (95%)
  local copies, waits for them, and re-layouts  1.25 us (3%)
  between operations  0.64 us (1%)
    pallas_call x1, Pallas kernels, body(): pl.pallas_call(kernel, out_shape=(jax.ShapeDtypeStruct((16, LOCAL), f32),...  43.5 us

profile of v9, /device:TPU:24, one launch (start us, length us, event | category | flops | bytes accessed | tf_op | source)
XLA Modules:
  0.0 45.4 jit_solution(7229570689904703869)
XLA Ops:
  0.6 43.5 %expectation.1 = (f32[16,4]{1,0:T(8,128)S(1)}, f32[16,36]{1,0:T(8,128)S(1)}) custom-call(bf16[18,128,128]{2,1,0:T(8,128)(2,1)} %constant.4.clone.cos_hbm, bf16[18,128,128]{2,1,0:T(8,128)(2,1)} %constant.5.clone.sin_hbm, f32[16,144]{1,0:T(8,128)} %images_hbm.1, bf16[4,9216]{1,0:T(4,128)(2,1)} %references_hbm.1, f32[32,32]{1,0:T(8,128)} %ctf_hbm.1, ...), custom_call_target="tpu_custom_call" | custom-call | tf_op jit(solution)/shard_map/expectation/pallas_call | solution.py:415
  44.2 0.7 %copy.11 = f32[16,4]{0,1:T(4,128)} copy(f32[16,4]{1,0:T(8,128)S(1)} %get-tuple-element.2) | data formatting | bytes 512 | tf_op jit(solution)/shard_map/expectation/pallas_call | solution.py:415
  44.8 0.6 %copy.13 = f32[16,36]{1,0:T(8,128)} copy(f32[16,36]{1,0:T(8,128)S(1)} %get-tuple-element.7) | data formatting | bytes 4608

commit v10 on v9

--- a/solution.py
+++ b/solution.py
@@ -240,6 +240,7 @@
 
     lax.fori_loop(0, HALF, arrange, 0)
 
+    relay_z(gathered, zsend, zrecv, x, z, z_copies)
     from_left.wait_recv()
     slot = rall.at[left, core]
     part = rall.at[left, core, part_a]
@@ -255,7 +256,6 @@
     onward_b.wait_recv()
     slot = rall.at[opposite, core]
     over_opposite = send(slot, slot, rsend.at[6], rrecv.at[6], me, ptl=sibling)
-    relay_z(gathered, zsend, zrecv, x, z, z_copies)
     over_left.wait_recv()
     place(left)
     over_right.wait_recv()

time: 45.6 us -> 46.8 us (1.026); the launches traced: 45.4 us -> 46.1 us
  Pallas kernels: 43.5 us -> 44.2 us
    pallas_call x1, Pallas kernels: 43.5 us -> 44.2 us  [body(): pl.pallas_call(kernel, out_shape=(jax.ShapeDtypeStruct((16, LOCAL), f32),...]
where the time goes in v10:
time: 46.8 us; the launch traced here: 46.1 us
  Pallas kernels  44.2 us (94%)
  local copies, waits for them, and re-layouts  1.25 us (3%)
  between operations  0.64 us (1%)
    pallas_call x1, Pallas kernels, body(): pl.pallas_call(kernel, out_shape=(jax.ShapeDtypeStruct((16, LOCAL), f32),...  44.2 us

profile of v10, /device:TPU:24, one launch (start us, length us, event | category | flops | bytes accessed | tf_op | source)
XLA Modules:
  0.0 46.1 jit_solution(6231953379815322103)
XLA Ops:
  0.6 44.2 %expectation.1 = (f32[16,4]{1,0:T(8,128)S(1)}, f32[16,36]{1,0:T(8,128)S(1)}) custom-call(bf16[18,128,128]{2,1,0:T(8,128)(2,1)} %constant.4.clone.cos_hbm, bf16[18,128,128]{2,1,0:T(8,128)(2,1)} %constant.5.clone.sin_hbm, f32[16,144]{1,0:T(8,128)} %images_hbm.1, bf16[4,9216]{1,0:T(4,128)(2,1)} %references_hbm.1, f32[32,32]{1,0:T(8,128)} %ctf_hbm.1, ...), custom_call_target="tpu_custom_call" | custom-call | tf_op jit(solution)/shard_map/expectation/pallas_call | solution.py:415
  44.8 0.7 %copy.11 = f32[16,4]{0,1:T(4,128)} copy(f32[16,4]{1,0:T(8,128)S(1)} %get-tuple-element.2) | data formatting | bytes 512 | tf_op jit(solution)/shard_map/expectation/pallas_call | solution.py:415
  45.5 0.6 %copy.13 = f32[16,36]{1,0:T(8,128)} copy(f32[16,36]{1,0:T(8,128)S(1)} %get-tuple-element.7) | data formatting | bytes 4608
